TPU v7x, 512 devices: a whole 4x8x8 slice. The times are simulated.
512 devices in a mesh: replica: 16 (over x, z_hi, core), fsdp: 32 (over y, z_lo).
Axes of the slice: x: 4, y: 8, z: 8 (z_hi: 2, z_lo: 4; z = z_hi * 4 + z_lo), core: 2. Of those that a mesh axis runs over, the one named last changes fastest.
Arguments:
- local_weights: bfloat16 [16, 2048, 8192], P('replica', 'fsdp'), may hold values from -12 to 12
- global_weights: bfloat16 [2048, 8192], P('fsdp'), may hold values from -4 to 4
- momentum: float32 [2048, 8192], P('fsdp', 'replica'), may hold values from -1.5 to 1.5
Outputs:
- new_weights: bfloat16 [2048, 8192], P('fsdp')
- new_momentum: float32 [2048, 8192], P('fsdp', 'replica')
All inputs are finite; a program needn't handle non-finite values. Where the computation divides by a largest or mean magnitude, that divisor is 1e-20 or more.
Results may differ from a plain program's by a relative error of at most 0.007.
Values may be sent and summed in bfloat16 or wider, within the bound.
No kernel may reach another device: no remote copies, remote signals or barrier semaphores. Data moves between devices by JAX's collectives and lax.ppermute only.
A program may use at most 64 MiB of HBM per device.

v0:
```python
import jax
import jax.numpy as jnp
from jax import lax
from jax.sharding import PartitionSpec as P

GROUP = 64


def group_codes(values):
    rows, cols = values.shape
    blocks = values.reshape(rows, cols // GROUP, GROUP)
    scale = (jnp.max(jnp.abs(blocks), axis=2) + 1e-06).astype(jnp.bfloat16)
    codes = (blocks / scale.astype(jnp.float32)[:, :, None]).astype(jnp.bfloat16)
    return (codes.reshape(rows, cols), scale)


def expand(codes, scale):
    rows, cols = codes.shape
    blocks = codes.reshape(rows, cols // GROUP, GROUP).astype(jnp.float32)
    return (blocks * scale.astype(jnp.float32)[:, :, None]).reshape(rows, cols)


def per_device(local_weights, global_weights, momentum):
    replicas = lax.axis_size("replica")
    base = global_weights.astype(jnp.float32)
    delta = local_weights[0].astype(jnp.float32) - base
    codes, scale = group_codes(delta)
    rows, width = delta.shape
    owned = width // replicas
    pieces = lax.axis_size("replica") * rows // rows
    values = expand(codes, scale).reshape(rows, pieces, owned)
    summed = lax.psum_scatter(
        jnp.transpose(values, (1, 0, 2)).reshape(pieces * rows, owned).astype(jnp.bfloat16),
        "replica",
        scatter_dimension=0,
        tiled=True,
    ).astype(jnp.float32)
    average = summed / replicas
    total = lax.psum(jnp.sum(average * average), ("replica", "fsdp"))
    entries = rows * width * lax.axis_size("fsdp")
    spread = jnp.sqrt(total / entries + 1e-06)
    factor = jnp.minimum(1.0, 0.04 / spread)
    clipped = factor * average
    new_momentum = 0.9 * momentum + clipped
    update = 0.7 * (clipped + 0.9 * new_momentum)
    update_codes, update_scale = group_codes(update)
    all_codes, all_scale = (
        lax.all_gather(update_codes, "replica", axis=1, tiled=True),
        lax.all_gather(update_scale, "replica", axis=1, tiled=True),
    )
    new_weights = (base - expand(all_codes, all_scale)).astype(jnp.bfloat16)
    return (new_weights, new_momentum)


def solution(mesh):
    in_specs = (P("replica", "fsdp", None), P("fsdp", None), P("fsdp", "replica"))
    out_specs = (P("fsdp", None), P("fsdp", "replica"))
    return jax.shard_map(
        per_device, mesh=mesh, in_specs=in_specs, out_specs=out_specs, check_vma=False
    )
```

profile of v0, /device:TPU:1, one launch (start us, length us, event | category | flops | bytes accessed | tf_op | source)
XLA Modules:
  0.0 290.6 jit_solution(16675055633282004111)
XLA Ops:
  7.2 0.0 reduce-scatter.2.cloned.1.call-start
  7.2 1.8 convert_subtract_fusion.1
  9.0 2.5 copy.17
  11.6 3.0 %abs.13 = f32[64,128,64]{2,1,0:T(8,128)} reshape(f32[64,8192]{1,0:T(8,128)S(1)} %get-tuple-element.5) | data formatting | bytes 4194304 | tf_op jit(solution)/shard_map/abs | solution.py:12
  14.6 3.3 %reduce_max.18 = f32[64,128]{1,0:T(8,128)S(1)} reduce(f32[64,128,64]{2,1,0:T(8,128)} %abs.13, f32[]{:T(128)} %constant.9.clone.1), dimensions={2}, to_apply=%region_0.0 | reduce | flops 516096 | bytes 2129924 | tf_op jit(solution)/shard_map/reduce_max | solution.py:12
  17.9 2.6 div.34
  20.5 3.4 %div.35 = f32[64,16,512]{2,1,0:T(8,128)S(1)} reshape(f32[64,128,64]{2,1,0:T(8,128)} %div.34) | data formatting | bytes 4194304 | tf_op jit(solution)/shard_map/div | solution.py:13
  23.9 2.1 fusion.2
  26.0 0.0 copy-start.2
  26.1 1.5 copy.13
  27.6 0.0 reduce-scatter.2.cloned.1.call-update
  27.6 0.0 all-gather.2.cloned.1.call-start
  27.7 92.6 %reduce-scatter.2.cloned.1.call-done = bf16[64,512]{1,0:T(8,128)(2,1)} async-done(((bf16[1024,512]{1,0:T(8,128)(2,1)}), bf16[64,512]{1,0:T(8,128)(2,1)}) %reduce-scatter.2.cloned.1.call-update) | async-done | bytes 65552 | tf_op jit(solution)/shard_map/reduce_scatter | solution.py:32
  120.3 1.5 fusion.7
  121.8 97.7 %psum.7 = f32[]{:T(128)} all-reduce(f32[]{:T(128)} %fusion.7), channel_id=1, replica_groups=mesh['replica'=16,'fsdp'=32] {'replica','fsdp'}, use_global_device_ids=true, to_apply=%region_3.0 | all-reduce | flops 1 | bytes 8 | tf_op jit(solution)/shard_map/psum | solution.py:39
  220.1 0.0 copy-done.2
  220.1 0.9 fusion.8
  221.0 0.0 copy-start.1
  221.0 0.1 abs.15
  221.1 0.1 reduce_max.19
  221.3 0.1 copy.14
  221.4 0.1 copy.15
  221.5 0.1 div.41
  221.6 0.1 div.42
  221.7 1.5 divide_convert_fusion
  223.2 0.0 all-gather.2.cloned.1.call-update
  223.2 26.7 %all_gather.7 = bf16[64,128]{0,1:T(8,128)(2,1)S(1)} all-gather(bf16[64,8]{0,1:T(8,128)(2,1)S(1)} %add_convert_fusion.1), channel_id=1, replica_groups=mesh['replica'=16,'fsdp'=32] {'replica'}, dimensions={1}, use_global_device_ids=true | all-gather | bytes 17408 | tf_op jit(solution)/shard_map/all_gather | solution.py:49
  249.9 0.1 copy.16
  250.0 2.6 mul.50
  252.6 0.0 copy-done.1
  252.6 0.0 copy-start
  252.6 3.6 %mul.51 = f32[64,8192]{1,0:T(8,128)S(1)} reshape(f32[64,128,64]{2,1,0:T(8,128)} %mul.50) | data formatting | bytes 4194304 | tf_op jit(solution)/shard_map/mul | solution.py:20
  256.2 25.1 %all-gather.2.cloned.1.call-done = bf16[64,8192]{1,0:T(8,128)(2,1)} async-done(((bf16[64,512]{1,0:T(8,128)(2,1)}), bf16[64,8192]{1,0:T(8,128)(2,1)}) %all-gather.2.cloned.1.call-update) | async-done | bytes 1048592 | tf_op jit(solution)/shard_map/all_gather | solution.py:48
  281.3 0.0 copy-done
  281.3 2.5 fusion
  (2 shorter events, 0.0 us)
Async XLA Ops:
  7.2 113.1 %reduce-scatter.2.cloned.1.call-start = ((), (), s32[]{:S(2)}) async-start(), calls=%async_computation.1 | async-start | bytes 1114112 | tf_op jit(solution)/shard_map/reduce_scatter | solution.py:32
  26.0 194.1 %copy-start.2 = (f32[64,512]{1,0:T(8,128)S(1)}, f32[64,512]{1,0:T(8,128)}, u32[]{:S(2)}) copy-start(f32[64,512]{1,0:T(8,128)} %param.5) | copy-start | bytes 393220
  27.6 253.7 %all-gather.2.cloned.1.call-start = ((), (), s32[]{:S(2)}) async-start(), calls=%async_computation.2 | async-start | bytes 1114112 | tf_op jit(solution)/shard_map/all_gather | solution.py:48
  221.0 31.5 %copy-start.1 = (f32[64,512]{1,0:T(8,128)}, f32[64,512]{1,0:T(8,128)S(1)}, u32[]{:S(2)}) copy-start(f32[64,512]{1,0:T(8,128)S(1)} %get-tuple-element.3) | copy-start | bytes 393220
  252.6 28.7 %copy-start = (bf16[64,8192]{1,0:T(8,128)(2,1)S(1)}, bf16[64,8192]{1,0:T(8,128)(2,1)}, u32[]{:S(2)}) copy-start(bf16[64,8192]{1,0:T(8,128)(2,1)} %param.4) | copy-start | bytes 3145732
Sparse Core Ops, SparseCore 0:
  27.7 92.4 reduce-scatter.1
  223.4 57.8 all-gather.1
where the time goes:
time: 291 us
  blocking collectives  124 us (43%)
  waiting for transfers between devices  118 us (41%)
  local copies, waits for them, and re-layouts  19.8 us (7%)
  between operations  14.8 us (5%)
  other arithmetic  13.8 us (5%)
    psum x1, blocking collectives, per_device(): total = lax.psum(jnp.sum(average * average), ('replica', 'fsdp'))  97.7 us
    reduce_scatter x1, waiting for transfers between devices, per_device(): lax.psum_scatter(jnp.transpose(values, (1, 0, 2)).reshape(pieces * rows,...  92.6 us
    all_gather x1, blocking collectives, per_device(): lax.all_gather(update_scale, 'replica', axis=1, tiled=True)  26.7 us
    all_gather x1, waiting for transfers between devices, per_device(): lax.all_gather(update_codes, 'replica', axis=1, tiled=True)  25.1 us
    div x4, local copies, waits for them, and re-layouts, group_codes(): blocks / scale.astype(jnp.float32)[:, :, None]  6.22 us
    mul x2, local copies, waits for them, and re-layouts, expand(): return (blocks * scale.astype(jnp.float32)[:, :, None]).reshape(rows, cols)  6.16 us
  transfers between devices with their start and end apart: 2, of which 2 were waited for; matrix products, arithmetic and copies ran while one was open for 2% of the time, Pallas kernels for 0%

commit v1 on v0

v1 whole, which is shorter than its diff:
```python
import jax
import jax.numpy as jnp
from jax import lax
from jax.experimental import pallas as pl
from jax.experimental.pallas import tpu as pltpu
from jax.sharding import Mesh, PartitionSpec as P

NX, NZ, NC, NY, NL = 4, 2, 2, 8, 4
REPLICAS = NX * NZ * NC
AXES = ("x", "zh", "c", "y", "zl")
REPLICA = ("x", "zh", "c")
FSDP = ("y", "zl")
OWN = 512
PAIR = NZ * OWN
F32, BF16 = jnp.float32, jnp.bfloat16
VMEM = pl.BlockSpec(memory_space=pltpu.VMEM)
SMEM = pl.BlockSpec(memory_space=pltpu.SMEM)


def block_cols(x, h, core):
    return pl.ds(pl.multiple_of(((x * NZ + h) * NC + core) * OWN, OWN), OWN)


def delta_kernel(flip, core_ref, *refs):
    out_ref = refs[-1]
    for h in range(NZ):
        delta = refs[h][0].astype(F32) - refs[NZ + h][...].astype(F32)
        out_ref[0, :, h * OWN:(h + 1) * OWN] = delta.astype(BF16)


def delta_half(core, local, base, name):
    rows = base.shape[0]

    def cols(h, lead):
        def index(i, s):
            return lead + (0, (i * NZ + h) * NC + s[0])
        return index

    return pl.pallas_call(
        lambda *refs: delta_kernel(None, *refs),
        grid_spec=pltpu.PrefetchScalarGridSpec(
            num_scalar_prefetch=1,
            grid=(NX,),
            in_specs=[pl.BlockSpec((1, rows, OWN), cols(h, (0,))) for h in range(NZ)]
            + [pl.BlockSpec((rows, OWN), cols(h, ())) for h in range(NZ)],
            out_specs=pl.BlockSpec((1, rows, PAIR), lambda i, s: (i, 0, 0)),
        ),
        out_shape=jax.ShapeDtypeStruct((NX, rows, PAIR), BF16),
        cost_estimate=pl.CostEstimate(flops=rows * 4096, bytes_accessed=6 * rows * 4096, transcendentals=0),
        name=name,
    )(core, local, local, base, base)


def quad_kernel(parts_ref, mom_ref, out_ref):
    total = parts_ref[0].astype(F32)
    for k in range(1, NX):
        total = total + parts_ref[k].astype(F32)
    out_ref[:, :PAIR] = total.astype(BF16)
    out_ref[:, PAIR:] = mom_ref[...].astype(BF16)


def total_kernel(both_ref, out_ref):
    total = (both_ref[0, :, :PAIR].astype(F32) + both_ref[1, :, :PAIR].astype(F32)).astype(BF16)
    for k in range(NX):
        out_ref[k, :, :PAIR] = total
        for h in range(NZ):
            out_ref[k, :, PAIR + h * OWN:PAIR + (h + 1) * OWN] = both_ref[h, :, PAIR:]


def squares_kernel(own_ref, out_ref):
    acc = jnp.zeros((own_ref.shape[1], 128), F32)
    for k in range(NX):
        for j in range(PAIR // 128):
            part = own_ref[k, :, j * 128:(j + 1) * 128].astype(F32)
            acc = acc + part * part
    out_ref[...] = jnp.broadcast_to(jnp.sum(acc), out_ref.shape)


def final_kernel(entries, core_ref, half_ref, shares_ref, base_ref, mom_ref, own_ref, other_ref, new_ref, newmom_ref):
    core = core_ref[0]
    half = half_ref[0]
    total = jnp.sum(shares_ref[...]) / (REPLICAS * REPLICAS)
    spread = jnp.sqrt(total / entries + 1e-06)
    factor = jnp.minimum(1.0, 0.04 / spread) / REPLICAS

    def part(which, src_ref):
        for x in range(NX):
            for h in range(NZ):
                cols = block_cols(x, h, which)
                clipped = factor * src_ref[x, :, h * OWN:(h + 1) * OWN].astype(F32)
                mom = 0.9 * src_ref[x, :, PAIR + h * OWN:PAIR + (h + 1) * OWN].astype(F32) + clipped
                update = 0.7 * (clipped + 0.9 * mom)
                new_ref[:, cols] = (base_ref[:, cols].astype(F32) - update).astype(BF16)

    part(core, own_ref)
    part(1 - core, other_ref)
    x = half_ref[1]
    cols = pl.ds(pl.multiple_of(half * OWN, OWN), OWN)
    newmom_ref[...] = 0.9 * mom_ref[...] + factor * own_ref[x, :, cols].astype(F32)


def per_device(local_weights, global_weights, momentum):
    rows, width = global_weights.shape
    core = lax.axis_index("c").astype(jnp.int32)
    half = lax.axis_index("zh").astype(jnp.int32)
    xi = lax.axis_index("x").astype(jnp.int32)
    swap = [(0, 1), (1, 0)]
    send = delta_half((1 - core).reshape(1), local_weights, global_weights, "delta_send")
    keep = delta_half(core.reshape(1), local_weights, global_weights, "delta_keep")
    pair = keep.astype(F32) + lax.ppermute(send, "c", swap).astype(F32)
    parts = lax.all_to_all(pair.astype(BF16), "x", 0, 0, tiled=True)
    quad = pl.pallas_call(
        quad_kernel, in_specs=[VMEM] * 2, out_specs=VMEM,
        out_shape=jax.ShapeDtypeStruct((rows, PAIR + OWN), BF16), name="quad",
    )(parts, momentum)
    both = lax.all_gather(quad, "zh", axis=0)
    total = pl.pallas_call(
        total_kernel, in_specs=[VMEM], out_specs=VMEM,
        out_shape=jax.ShapeDtypeStruct((NX, rows, 2 * PAIR), BF16), name="total",
    )(both)
    own = lax.all_to_all(total, "x", 0, 0, tiled=True)
    other = lax.ppermute(own, "c", swap)
    group = NC * NY * NL
    squares = pl.pallas_call(
        squares_kernel, in_specs=[VMEM], out_specs=VMEM,
        out_shape=jax.ShapeDtypeStruct((group, 1), F32), name="squares",
    )(own)
    shares = lax.all_to_all(squares, ("c", "y", "zl"), 0, 0, tiled=True)
    entries = rows * width * NY * NL
    new_weights, new_momentum = pl.pallas_call(
        lambda *refs: final_kernel(entries, *refs),
        in_specs=[SMEM, SMEM] + [VMEM] * 5, out_specs=[VMEM, VMEM],
        out_shape=[jax.ShapeDtypeStruct((rows, width), BF16), jax.ShapeDtypeStruct(momentum.shape, F32)],
        name="final",
    )(core.reshape(1), jnp.stack([half, xi]), shares, global_weights, momentum, own, other)
    return (new_weights, new_momentum)


def solution(mesh):
    fine = Mesh(mesh.devices.reshape(NX, NZ, NC, NY, NL), AXES)
    in_specs = (P(REPLICA, FSDP, None), P(FSDP, None), P(FSDP, REPLICA))
    out_specs = (P(FSDP, None), P(FSDP, REPLICA))
    return jax.shard_map(
        per_device, mesh=fine, in_specs=in_specs, out_specs=out_specs, check_vma=False
    )
```

time: 291 us -> 98.1 us (0.34)
  waiting for transfers between devices: 118 us -> 8.67 us
  blocking collectives: 124 us -> 40.1 us
  starting transfers between devices: 0.08 us -> 28.6 us
  local copies, waits for them, and re-layouts: 19.8 us -> 1.05 us
  Pallas kernels: 0 us -> 16.4 us
  between operations: 14.8 us -> 0.69 us
  other arithmetic: 13.8 us -> 1.87 us
    psum x1 -> x0, blocking collectives: 97.7 us -> none  [per_device(): total = lax.psum(jnp.sum(average * average), ('replica', 'fsdp'))]
    reduce_scatter x1 -> x0, waiting for transfers between devices: 92.6 us -> none  [per_device(): lax.psum_scatter(jnp.transpose(values, (1, 0, 2)).reshape(pieces * rows,...]
    all_to_all x0 -> x2, blocking collectives: none -> 29.2 us  [the longest x1 16.8 us: per_device(): own = lax.all_to_all(total, 'x', 0, 0, tiled=True)]
    all_gather x1 -> x0, waiting for transfers between devices: 25.1 us -> none  [per_device(): lax.all_gather(update_codes, 'replica', axis=1, tiled=True)]
    pallas_call x0 -> x6, Pallas kernels: none -> 16.4 us  [the longest x2 6.61 us: delta_half(): pl.pallas_call(lambda *refs: delta_kernel(None, *refs), grid_spec=pltpu.P...]
    all_gather x1, blocking collectives: 26.7 us -> 10.9 us  [per_device(): both = lax.all_gather(quad, 'zh', axis=0)]
    all_to_all x0 -> x1, starting transfers between devices: none -> 15.1 us  [per_device(): shares = lax.all_to_all(squares, ('c', 'y', 'zl'), 0, 0, tiled=True)]
    ppermute x0 -> x2, starting transfers between devices: none -> 13.4 us  [the longest x1 8.77 us: per_device(): pair = keep.astype(F32) + lax.ppermute(send, 'c', swap).astype(F32)]
  transfers between devices with their start and end apart: 2 -> 3, of which waited for: 2 -> 1; matrix products, arithmetic and copies ran while one was open for 2% -> 1% of each run, Pallas kernels for 0% -> 6%
where the time goes in v1:
time: 98.1 us; the launch traced here: 97.2 us
  blocking collectives  40.1 us (41%)
  starting transfers between devices  28.6 us (29%)
  Pallas kernels  16.4 us (17%)
  waiting for transfers between devices  8.67 us (9%)
  other arithmetic  1.87 us (2%)
  local copies, waits for them, and re-layouts  1.05 us (1%)
    all_to_all x1, blocking collectives, per_device(): own = lax.all_to_all(total, 'x', 0, 0, tiled=True)  16.8 us
    all_to_all x1, starting transfers between devices, per_device(): shares = lax.all_to_all(squares, ('c', 'y', 'zl'), 0, 0, tiled=True)  15.1 us
    all_to_all x1, blocking collectives, per_device(): parts = lax.all_to_all(pair.astype(BF16), 'x', 0, 0, tiled=True)  12.4 us
    all_gather x1, blocking collectives, per_device(): both = lax.all_gather(quad, 'zh', axis=0)  10.9 us
    ppermute x1, starting transfers between devices, per_device(): pair = keep.astype(F32) + lax.ppermute(send, 'c', swap).astype(F32)  8.77 us
    all_to_all x1, waiting for transfers between devices, per_device(): shares = lax.all_to_all(squares, ('c', 'y', 'zl'), 0, 0, tiled=True)  8.66 us
    pallas_call x2, Pallas kernels, delta_half(): pl.pallas_call(lambda *refs: delta_kernel(None, *refs), grid_spec=pltpu.P...  6.61 us
    ppermute x1, starting transfers between devices, per_device(): other = lax.ppermute(own, 'c', swap)  4.66 us
  transfers between devices with their start and end apart: 3, of which 1 were waited for; matrix products, arithmetic and copies ran while one was open for 1% of the time, Pallas kernels for 6%

profile of v1, /device:TPU:1, one launch (start us, length us, event | category | flops | bytes accessed | tf_op | source)
XLA Modules:
  0.0 97.2 jit_solution(5635455042077669709)
XLA Ops:
  0.6 3.3 %delta_send.1 = bf16[4,64,1024]{2,1,0:T(8,128)(2,1)} custom-call(s32[1]{0:T(128)} %bitcast.3.refs_0_, bf16[1,64,8192]{2,1,0:T(8,128)(2,1)} %refs_2_.3, bf16[1,64,8192]{2,1,0:T(8,128)(2,1)} %refs_2_.3, bf16[64,8192]{1,0:T(8,128)(2,1)} %refs_3_.5, bf16[64,8192]{1,0:T(8,128)(2,1)} %refs_3_.5), custom_call_target="tpu_custom_call" | custom-call | flops 262144 | bytes 1572864 | tf_op jit(solution)/shard_map/delta_send/pallas_call | solution.py:39
  3.9 8.8 %collective-permute-start = (bf16[4,64,1024]{2,1,0:T(8,128)(2,1)}, bf16[4,64,1024]{2,1,0:T(8,128)(2,1)S(1)}, u32[]{:S(2)}, u32[]{:S(2)}) collective-permute-start(bf16[4,64,1024]{2,1,0:T(8,128)(2,1)} %delta_send.1), channel_id=1, source_target_pairs={{0,32},{32,0},{1,33},{33,1},{2,34},{34,2},{3,35},{35,3},{4,36},{36... | collective-permute-start | bytes 1572872 | tf_op jit(solution)/shard_map/ppermute | solution.py:110
  12.7 3.3 %delta_keep.1 = bf16[4,64,1024]{2,1,0:T(8,128)(2,1)} custom-call(s32[1]{0:T(128)} %bitcast.refs_0_, bf16[1,64,8192]{2,1,0:T(8,128)(2,1)} %refs_2_.3, bf16[1,64,8192]{2,1,0:T(8,128)(2,1)} %refs_2_.3, bf16[64,8192]{1,0:T(8,128)(2,1)} %refs_3_.5, bf16[64,8192]{1,0:T(8,128)(2,1)} %refs_3_.5), custom_call_target="tpu_custom_call" | custom-call | flops 262144 | bytes 1572864 | tf_op jit(solution)/shard_map/delta_keep/pallas_call | solution.py:39
  16.0 0.0 collective-permute-done
  16.0 1.2 %add_convert_fusion = bf16[4,64,1024]{2,1,0:T(8,128)(2,1)S(1)} fusion(bf16[4,64,1024]{2,1,0:T(8,128)(2,1)S(1)} %collective-permute-done, bf16[4,64,1024]{2,1,0:T(8,128)(2,1)} %delta_keep.1), kind=kLoop, calls=%fused_computation | loop fusion | flops 1048576 | bytes 1572864 | tf_op jit(solution)/shard_map/convert_element_type | solution.py:111
  17.3 12.4 %all_to_all.21.parts_ref = bf16[4,64,1024]{2,1,0:T(8,128)(2,1)} all-to-all(bf16[4,64,1024]{2,1,0:T(8,128)(2,1)S(1)} %add_convert_fusion), channel_id=1, replica_groups=mesh['x'=4,'zh'=2,'c'=2,'y'=8,'zl'=4] {'x'}, dimensions={0} | all-to-all | bytes 1048576 | tf_op jit(solution)/shard_map/all_to_all | solution.py:111
  29.7 1.8 %quad.1 = bf16[64,1536]{1,0:T(8,128)(2,1)} custom-call(bf16[4,64,1024]{2,1,0:T(8,128)(2,1)} %all_to_all.21.parts_ref, f32[64,512]{1,0:T(8,128)} %refs_4_.5), custom_call_target="tpu_custom_call" | custom-call | tf_op jit(solution)/shard_map/quad/pallas_call | solution.py:112
  31.5 10.9 %all-gather = bf16[128,1536]{1,0:T(8,128)(2,1)} all-gather(bf16[64,1536]{1,0:T(8,128)(2,1)} %quad.1), channel_id=2, replica_groups=mesh['x'=4,'zh'=2,'c'=2,'y'=8,'zl'=4] {'zh'}, dimensions={0}, use_global_device_ids=true | all-gather | bytes 589824 | tf_op jit(solution)/shard_map/all_gather | solution.py:116
  42.4 2.0 %total.1 = bf16[4,64,2048]{2,1,0:T(8,128)(2,1)} custom-call(bf16[2,64,1536]{2,1,0:T(8,128)(2,1)} %bitcast.7), custom_call_target="tpu_custom_call" | custom-call | tf_op jit(solution)/shard_map/total/pallas_call | solution.py:117
  44.4 16.8 %all_to_all.22.own_ref.refs_5_ = bf16[4,64,2048]{2,1,0:T(8,128)(2,1)S(1)} all-to-all(bf16[4,64,2048]{2,1,0:T(8,128)(2,1)} %total.1), channel_id=1, replica_groups=mesh['x'=4,'zh'=2,'c'=2,'y'=8,'zl'=4] {'x'}, dimensions={0} | all-to-all | bytes 2097152 | tf_op jit(solution)/shard_map/all_to_all | solution.py:121
  61.2 0.0 copy-start
  61.2 4.7 %collective-permute-start.1 = (bf16[4,64,2048]{2,1,0:T(8,128)(2,1)S(1)}, bf16[4,64,2048]{2,1,0:T(8,128)(2,1)S(1)}, u32[]{:S(2)}, u32[]{:S(2)}) collective-permute-start(bf16[4,64,2048]{2,1,0:T(8,128)(2,1)S(1)} %all_to_all.22.own_ref.refs_5_), channel_id=1, source_target_pairs={{0,32},{32,0},{1,33},{33,1},{2,34},{34,2},{3,35},{35,3},{4,36},{36... | collective-permute-start | bytes 3145736 | tf_op jit(solution)/shard_map/ppermute | solution.py:122
  65.9 0.0 copy-done
  65.9 2.1 %squares.1 = f32[64,1]{1,0:T(8,128)} custom-call(bf16[4,64,2048]{2,1,0:T(8,128)(2,1)} %copy-done), custom_call_target="tpu_custom_call" | custom-call | tf_op jit(solution)/shard_map/squares/pallas_call | solution.py:124
  67.9 15.1 %all-to-all-start.2 = ((f32[64,1,1]{2,1,0:T(1,128)}), f32[64,1,1]{2,1,0:T(1,128)S(1)}, u32[]{:S(2)}, u32[]{:S(2)}) async-start(f32[64,1,1]{2,1,0:T(1,128)} %bitcast.9), calls=%async_computation.2 | async-start | bytes 65536 | tf_op jit(solution)/shard_map/all_to_all | solution.py:128
  83.1 0.6 pad_add_fusion.refs_1_
  83.7 8.7 %all-to-all-done.2 = f32[64,1,1]{2,1,0:T(1,128)S(1)} async-done(((f32[64,1,1]{2,1,0:T(1,128)}), f32[64,1,1]{2,1,0:T(1,128)S(1)}, u32[]{:S(2)}, u32[]{:S(2)}) %all-to-all-start.2) | async-done | bytes 288 | tf_op jit(solution)/shard_map/all_to_all | solution.py:128
  92.4 0.0 copy-start.2
  92.4 0.0 collective-permute-done.1.refs_6_
  92.4 0.0 copy-start.1
  92.4 0.6 copy-done.2
  93.0 0.4 copy-done.1
  93.4 3.8 %final.1 = (bf16[64,8192]{1,0:T(8,128)(2,1)}, f32[64,512]{1,0:T(8,128)}) custom-call(s32[1]{0:T(128)} %bitcast.refs_0_, s32[2]{0:T(128)} %pad_add_fusion.refs_1_, f32[64,1]{1,0:T(8,128)} %bitcast.8, bf16[64,8192]{1,0:T(8,128)(2,1)} %refs_3_.5, f32[64,512]{1,0:T(8,128)} %refs_4_.5, bf16[4,64,2048]{2,1,0:T(8,128)(2,1)} %copy-done, bf16[4,64,2048]{2,1,0:T(8,128)(2,1)} %copy-done.1), custom_call_target="tpu_custom_call" | custom-call | tf_op jit(solution)/shard_map/final/pallas_call | solution.py:130
Async XLA Ops:
  3.9 12.1 %collective-permute-start = (bf16[4,64,1024]{2,1,0:T(8,128)(2,1)}, bf16[4,64,1024]{2,1,0:T(8,128)(2,1)S(1)}, u32[]{:S(2)}, u32[]{:S(2)}) collective-permute-start(bf16[4,64,1024]{2,1,0:T(8,128)(2,1)} %delta_send.1), channel_id=1, source_target_pairs={{0,32},{32,0},{1,33},{33,1},{2,34},{34,2},{3,35},{35,3},{4,36},{36... | collective-permute-start | bytes 1572872 | tf_op jit(solution)/shard_map/ppermute | solution.py:110
  61.2 4.7 %copy-start = (bf16[4,64,2048]{2,1,0:T(8,128)(2,1)}, bf16[4,64,2048]{2,1,0:T(8,128)(2,1)S(1)}, u32[]{:S(2)}) copy-start(bf16[4,64,2048]{2,1,0:T(8,128)(2,1)S(1)} %all_to_all.22.own_ref.refs_5_) | copy-start | bytes 3145732
  61.2 31.2 %collective-permute-start.1 = (bf16[4,64,2048]{2,1,0:T(8,128)(2,1)S(1)}, bf16[4,64,2048]{2,1,0:T(8,128)(2,1)S(1)}, u32[]{:S(2)}, u32[]{:S(2)}) collective-permute-start(bf16[4,64,2048]{2,1,0:T(8,128)(2,1)S(1)} %all_to_all.22.own_ref.refs_5_), channel_id=1, source_target_pairs={{0,32},{32,0},{1,33},{33,1},{2,34},{34,2},{3,35},{35,3},{4,36},{36... | collective-permute-start | bytes 3145736 | tf_op jit(solution)/shard_map/ppermute | solution.py:122
  67.9 24.4 %all-to-all-start.2 = ((f32[64,1,1]{2,1,0:T(1,128)}), f32[64,1,1]{2,1,0:T(1,128)S(1)}, u32[]{:S(2)}, u32[]{:S(2)}) async-start(f32[64,1,1]{2,1,0:T(1,128)} %bitcast.9), calls=%async_computation.2 | async-start | bytes 65536 | tf_op jit(solution)/shard_map/all_to_all | solution.py:128
  92.4 0.6 copy-start.2
  92.4 1.0 %copy-start.1 = (bf16[4,64,2048]{2,1,0:T(8,128)(2,1)}, bf16[4,64,2048]{2,1,0:T(8,128)(2,1)S(1)}, u32[]{:S(2)}) copy-start(bf16[4,64,2048]{2,1,0:T(8,128)(2,1)S(1)} %collective-permute-done.1.refs_6_) | copy-start | bytes 3145732

commit v2 on v0

v2 whole, which is shorter than its diff:
```python
import jax
import jax.numpy as jnp
from jax import lax
from jax.experimental import pallas as pl
from jax.experimental.pallas import tpu as pltpu
from jax.sharding import Mesh, PartitionSpec as P

NX, NZ, NC, NY, NL = 4, 2, 2, 8, 4
AXES = ("x", "zh", "c", "y", "zl")
REPLICA = ("x", "zh", "c")
FSDP = ("y", "zl")
REPLICAS = NX * NZ * NC
ROWS = 64
OWN = 512
LANES = 128
TILES = OWN // LANES
SUMS = NZ * TILES * ROWS
MOM = TILES * ROWS
REST = 16
MOST = MOM - REST
QUAD = SUMS + MOST + NX * REST
GATHER = SUMS + NZ * MOST
F32, BF16 = jnp.float32, jnp.bfloat16
VMEM = pl.BlockSpec(memory_space=pltpu.VMEM)
HBM = pl.BlockSpec(memory_space=pl.ANY)
SMALL = pltpu.CompilerParams(vmem_limit_bytes=4 * 1024 * 1024)


def near(x):
    return pltpu.with_memory_space_constraint(x, pltpu.VMEM)


def far(x):
    return pltpu.with_memory_space_constraint(x, pltpu.HBM)


def flat(tile):
    return slice(tile * ROWS, (tile + 1) * ROWS)


def block_cols(x, h, core):
    return pl.ds(pl.multiple_of(((x * NZ + h) * NC + core) * OWN, OWN), OWN)


def delta_kernel(own, local_ref, base_ref, *refs):
    out_ref, local_buf, base_buf, sems = refs[-4:]
    core = lax.axis_index("c")
    core = core if own else 1 - core
    copies = []
    for x in range(NX):
        for h in range(NZ):
            cols = block_cols(x, h, core)
            to = slice(h * OWN, (h + 1) * OWN)
            pair = [
                pltpu.make_async_copy(local_ref.at[0, :, cols], local_buf.at[x, :, to], sems.at[0, x, h]),
                pltpu.make_async_copy(base_ref.at[:, cols], base_buf.at[x, :, to], sems.at[1, x, h]),
            ]
            for copy in pair:
                copy.start()
            copies.append((x, h, pair))
    rest = jnp.zeros((REST, LANES), BF16)
    if own:
        rest = refs[0][ROWS - REST:, OWN - LANES:].astype(BF16)
    for x in range(NX):
        out_ref[x, SUMS:, :] = rest
    for x, h, pair in copies:
        for copy in pair:
            copy.wait()
        for t in range(TILES):
            cols = slice(h * OWN + t * LANES, h * OWN + (t + 1) * LANES)
            delta = local_buf[x, :, cols].astype(F32) - base_buf[x, :, cols].astype(F32)
            out_ref[x, flat(h * TILES + t), :] = delta.astype(BF16)


def delta_half(own, local, base, momentum, name):
    buf = pltpu.VMEM((NX, ROWS, NZ * OWN), BF16)
    return pl.pallas_call(
        lambda *refs: delta_kernel(own, *refs),
        in_specs=[HBM, HBM] + [VMEM] * own,
        out_specs=VMEM,
        out_shape=pltpu.VMEM((NX, SUMS + REST, LANES), BF16),
        scratch_shapes=[buf, buf, pltpu.SemaphoreType.DMA((2, NX, NZ))],
        cost_estimate=pl.CostEstimate(flops=2**18, bytes_accessed=3 * 2**19, transcendentals=0),
        compiler_params=SMALL,
        name=name,
    )(far(local), far(base), *([near(momentum)] if own else []))


def quad_kernel(parts_ref, mom_ref, out_ref):
    for t in range(NZ * TILES):
        total = parts_ref[0, flat(t), :].astype(F32)
        for k in range(1, NX):
            total = total + parts_ref[k, flat(t), :].astype(F32)
        out_ref[flat(t), :] = total.astype(BF16)
    for t in range(TILES):
        rows = ROWS - REST if t == TILES - 1 else ROWS
        at = SUMS + t * ROWS
        out_ref[at:at + rows, :] = mom_ref[:rows, t * LANES:(t + 1) * LANES].astype(BF16)
    for k in range(NX):
        at = SUMS + MOST + k * REST
        out_ref[at:at + REST, :] = parts_ref[k, SUMS:, :]


def total_kernel(both_ref, out_ref, squares_ref):
    acc = jnp.zeros((ROWS, LANES), F32)
    for t in range(NZ * TILES):
        total = both_ref[0, flat(t), :].astype(F32) + both_ref[1, flat(t), :].astype(F32)
        total = total.astype(BF16)
        out_ref[flat(t), :] = total
        acc = acc + total.astype(F32) * total.astype(F32)
    for h in range(NZ):
        at = SUMS + h * MOST
        out_ref[at:at + MOST, :] = both_ref[h, SUMS:SUMS + MOST, :]
    squares_ref[...] = jnp.broadcast_to(jnp.sum(acc), squares_ref.shape)


def pack_kernel(shares_ref, both_ref, out_ref):
    for h in range(NZ):
        out_ref[flat(h), :] = both_ref[h, SUMS + MOST:, :].astype(F32)
    out_ref[NZ * ROWS:, :] = jnp.broadcast_to(jnp.sum(shares_ref[:, 0:1]), (8, LANES))


def final_kernel(entries, pack_refs, base_ref, mom_ref, sum_refs, new_ref, newmom_ref, buf, sems):
    core = lax.axis_index("c")
    squares = pack_refs[0][NZ * ROWS:, :] + pack_refs[1][NZ * ROWS:, :]
    mean = jnp.sum(squares[0:1, 0:1]) / (REPLICAS * REPLICAS) / entries
    factor = jnp.minimum(1.0, 0.04 / jnp.sqrt(mean + 1e-06)) / REPLICAS

    def weights(rows, cols, total, mom):
        clipped = factor * total.astype(F32)
        update = 0.7 * (clipped + 0.9 * (0.9 * mom.astype(F32) + clipped))
        buf[rows, cols] = (base_ref[rows, cols].astype(F32) - update).astype(BF16)

    copies = []
    for x in range(NX):
        for which in range(NC):
            sums, pack = sum_refs[which], pack_refs[which]
            owner = core if which == 0 else 1 - core
            for h in range(NZ):
                for t in range(TILES):
                    start = ((x * NZ + h) * NC + owner) * OWN + t * LANES
                    cols = pl.ds(pl.multiple_of(start, LANES), LANES)
                    at = (h * TILES + t) * ROWS
                    mom_at = SUMS + h * MOST + t * ROWS
                    rows = ROWS - REST if t == TILES - 1 else ROWS
                    weights(slice(0, rows), cols, sums[x, at:at + rows, :], sums[x, mom_at:mom_at + rows, :])
                    if rows < ROWS:
                        rest_at = h * ROWS + x * REST
                        weights(slice(rows, ROWS), cols, sums[x, at + rows:at + ROWS, :], pack[rest_at:rest_at + REST, :])
        cols = slice(x * NZ * NC * OWN, (x + 1) * NZ * NC * OWN)
        copies.append(pltpu.make_async_copy(buf.at[:, cols], new_ref.at[:, cols], sems.at[x]))
        copies[-1].start()
    for t in range(TILES):
        at = pl.multiple_of((lax.axis_index("zh") * TILES + t) * ROWS, ROWS)
        total = sum_refs[0][lax.axis_index("x"), pl.ds(at, ROWS), :].astype(F32)
        cols = slice(t * LANES, (t + 1) * LANES)
        newmom_ref[:, cols] = 0.9 * mom_ref[:, cols] + factor * total
    for copy in copies:
        copy.wait()


def per_device(local_weights, global_weights, momentum):
    rows, width = global_weights.shape
    swap = [(0, 1), (1, 0)]
    send = delta_half(False, local_weights, global_weights, momentum, "delta_send")
    keep = delta_half(True, local_weights, global_weights, momentum, "delta_keep")
    pair = (keep.astype(F32) + lax.ppermute(send, "c", swap).astype(F32)).astype(BF16)
    parts = lax.all_to_all(pair, "x", 0, 0, tiled=True)
    quad = pl.pallas_call(
        quad_kernel, in_specs=[VMEM] * 2, out_specs=VMEM, out_shape=pltpu.VMEM((QUAD, LANES), BF16),
        compiler_params=SMALL, name="quad",
    )(near(parts), near(momentum))
    both = lax.all_gather(quad, "zh", axis=0)
    group = NX * NY * NL
    total, squares = pl.pallas_call(
        total_kernel, in_specs=[VMEM], out_specs=[VMEM, VMEM],
        out_shape=[pltpu.VMEM((GATHER, LANES), BF16), pltpu.VMEM((group, 2), F32)],
        compiler_params=SMALL, name="total",
    )(near(both))
    shares = lax.all_to_all(squares, ("x", "y", "zl"), 0, 0, tiled=True)
    own = lax.all_gather(total, "x", axis=0)
    other = lax.ppermute(lax.optimization_barrier((own, shares))[0], "c", swap)
    pack = pl.pallas_call(
        pack_kernel, in_specs=[VMEM] * 2, out_specs=VMEM,
        out_shape=pltpu.VMEM((NZ * ROWS + 8, LANES), F32),
        compiler_params=SMALL, name="pack",
    )(near(shares), near(both))
    other_pack = lax.ppermute(pack, "c", swap)
    entries = rows * width * NY * NL
    return pl.pallas_call(
        lambda p0, p1, base, mom, s0, s1, *refs: final_kernel(entries, (p0, p1), base, mom, (s0, s1), *refs),
        in_specs=[VMEM] * 6, out_specs=[HBM, VMEM],
        out_shape=[jax.ShapeDtypeStruct((rows, width), BF16), jax.ShapeDtypeStruct(momentum.shape, F32)],
        scratch_shapes=[pltpu.VMEM((rows, width), BF16), pltpu.SemaphoreType.DMA((NX,))],
        compiler_params=SMALL, name="final",
    )(near(pack), near(other_pack), near(global_weights), near(momentum), near(own), near(other))


def solution(mesh):
    fine = Mesh(mesh.devices.reshape(NX, NZ, NC, NY, NL), AXES)
    in_specs = (P(REPLICA, FSDP, None), P(FSDP, None), P(FSDP, REPLICA))
    out_specs = (P(FSDP, None), P(FSDP, REPLICA))
    return jax.shard_map(
        per_device, mesh=fine, in_specs=in_specs, out_specs=out_specs, check_vma=False
    )
```

time: 291 us -> 75.5 us (0.26)
  waiting for transfers between devices: 118 us -> 1.34 us
  blocking collectives: 124 us -> 35.5 us
  starting transfers between devices: 0.08 us -> 31.3 us
  local copies, waits for them, and re-layouts: 19.8 us -> 0.01 us
  between operations: 14.8 us -> 0.71 us
  other arithmetic: 13.8 us -> 0.14 us
  Pallas kernels: 0 us -> 6.11 us
    psum x1 -> x0, blocking collectives: 97.7 us -> none  [per_device(): total = lax.psum(jnp.sum(average * average), ('replica', 'fsdp'))]
    reduce_scatter x1 -> x0, waiting for transfers between devices: 92.6 us -> none  [per_device(): lax.psum_scatter(jnp.transpose(values, (1, 0, 2)).reshape(pieces * rows,...]
    all_gather x1 -> x0, waiting for transfers between devices: 25.1 us -> none  [per_device(): lax.all_gather(update_codes, 'replica', axis=1, tiled=True)]
    all_to_all x0 -> x1, starting transfers between devices: none -> 16.8 us  [per_device(): shares = lax.all_to_all(squares, ('x', 'y', 'zl'), 0, 0, tiled=True)]
    ppermute x0 -> x3, starting transfers between devices: none -> 14.5 us  [the longest x1 8.79 us: per_device(): lax.ppermute(send, 'c', swap).astype(F32)]
    all_to_all x0 -> x1, blocking collectives: none -> 11.8 us  [per_device(): parts = lax.all_to_all(pair, 'x', 0, 0, tiled=True)]
    div x4 -> x0, local copies, waits for them, and re-layouts: 6.22 us -> none  [group_codes(): blocks / scale.astype(jnp.float32)[:, :, None]]
    mul x2 -> x0, local copies, waits for them, and re-layouts: 6.16 us -> none  [expand(): return (blocks * scale.astype(jnp.float32)[:, :, None]).reshape(rows, cols)]
  transfers between devices with their start and end apart: 2 -> 4, of which waited for: 2 -> 2; matrix products, arithmetic and copies ran while one was open for 2% -> 0% of each run, Pallas kernels for 0% -> 2%
where the time goes in v2:
time: 75.5 us; the launch traced here: 75.1 us
  blocking collectives  35.5 us (47%)
  starting transfers between devices  31.3 us (41%)
  Pallas kernels  6.11 us (8%)
  waiting for transfers between devices  1.34 us (2%)
    all_to_all x1, starting transfers between devices, per_device(): shares = lax.all_to_all(squares, ('x', 'y', 'zl'), 0, 0, tiled=True)  16.8 us
    all_gather x1, blocking collectives, per_device(): own = lax.all_gather(total, 'x', axis=0)  13.7 us
    all_to_all x1, blocking collectives, per_device(): parts = lax.all_to_all(pair, 'x', 0, 0, tiled=True)  11.8 us
    all_gather x1, blocking collectives, per_device(): both = lax.all_gather(quad, 'zh', axis=0)  10 us
    ppermute x1, starting transfers between devices, per_device(): lax.ppermute(send, 'c', swap).astype(F32)  8.79 us
    ppermute x1, starting transfers between devices, per_device(): other = lax.ppermute(lax.optimization_barrier((own, shares))[0], 'c', swap)  3.83 us
    pallas_call x2, Pallas kernels, delta_half(): pl.pallas_call(lambda *refs: delta_kernel(own, *refs), in_specs=[HBM, HBM...  2.85 us
    pallas_call x1, Pallas kernels, per_device(): pl.pallas_call(lambda p0, p1, base, mom, s0, s1, *refs: final_kernel(entr...  2.26 us
  transfers between devices with their start and end apart: 4, of which 2 were waited for; matrix products, arithmetic and copies ran while one was open for 0% of the time, Pallas kernels for 2%

profile of v2, /device:TPU:1, one launch (start us, length us, event | category | flops | bytes accessed | tf_op | source)
XLA Modules:
  0.0 75.1 jit_solution(16630452790184500637)
XLA Ops:
  0.6 0.0 copy-start.1
  0.6 1.4 %delta_send.1 = bf16[4,528,128]{2,1,0:T(8,128)(2,1)S(1)} custom-call(bf16[1,64,8192]{2,1,0:T(8,128)(2,1)} %refs_0_.3, bf16[64,8192]{1,0:T(8,128)(2,1)} %base.1), custom_call_target="tpu_custom_call" | custom-call | flops 262144 | bytes 1572864 | tf_op jit(solution)/shard_map/delta_send/pallas_call | solution.py:77
  2.1 8.8 %collective-permute-start = (bf16[4,528,128]{2,1,0:T(8,128)(2,1)S(1)}, bf16[4,528,128]{2,1,0:T(8,128)(2,1)S(1)}, u32[]{:S(2)}, u32[]{:S(2)}) collective-permute-start(bf16[4,528,128]{2,1,0:T(8,128)(2,1)S(1)} %delta_send.1), channel_id=1, source_target_pairs={{0,32},{32,0},{1,33},{33,1},{2,34},{34,2},{3,35},{35,3},{4,36},{36... | collective-permute-start | bytes 1622024 | tf_op jit(solution)/shard_map/ppermute | solution.py:167
  10.9 0.0 copy-done.1
  10.9 1.4 %delta_keep.1 = bf16[4,528,128]{2,1,0:T(8,128)(2,1)S(1)} custom-call(bf16[1,64,8192]{2,1,0:T(8,128)(2,1)} %refs_0_.3, bf16[64,8192]{1,0:T(8,128)(2,1)} %base.1, f32[64,512]{1,0:T(8,128)S(1)} %copy-done.1), custom_call_target="tpu_custom_call" | custom-call | flops 262144 | bytes 1572864 | tf_op jit(solution)/shard_map/delta_keep/pallas_call | solution.py:77
  12.3 0.1 collective-permute-done
  12.4 0.1 add_convert_fusion
  12.6 11.8 %all_to_all.16.parts_ref = bf16[4,528,128]{2,1,0:T(8,128)(2,1)S(1)} all-to-all(bf16[4,528,128]{2,1,0:T(8,128)(2,1)S(1)} %add_convert_fusion), channel_id=1, replica_groups=mesh['x'=4,'zh'=2,'c'=2,'y'=8,'zl'=4] {'x'}, dimensions={0} | all-to-all | bytes 1081344 | tf_op jit(solution)/shard_map/all_to_all | solution.py:168
  24.3 0.1 quad.1
  24.4 10.0 %all-gather = bf16[1632,128]{1,0:T(8,128)(2,1)S(1)} all-gather(bf16[816,128]{1,0:T(8,128)(2,1)S(1)} %quad.1), channel_id=2, replica_groups=mesh['x'=4,'zh'=2,'c'=2,'y'=8,'zl'=4] {'zh'}, dimensions={0}, use_global_device_ids=true | all-gather | bytes 626688 | tf_op jit(solution)/shard_map/all_gather | solution.py:173
  34.5 0.8 %total.1 = (bf16[992,128]{1,0:T(8,128)(2,1)S(1)}, f32[128,2]{1,0:T(8,128)}) custom-call(bf16[2,816,128]{2,1,0:T(8,128)(2,1)S(1)} %bitcast.8), custom_call_target="tpu_custom_call" | custom-call | tf_op jit(solution)/shard_map/total/pallas_call | solution.py:175
  35.2 0.0 copy-start
  35.3 16.8 %all-to-all-start.1 = ((f32[128,1,2]{2,1,0:T(1,128)}), f32[128,1,2]{2,1,0:T(1,128)S(1)}, u32[]{:S(2)}, u32[]{:S(2)}) async-start(f32[128,1,2]{2,1,0:T(1,128)} %bitcast.2), calls=%async_computation.1 | async-start | bytes 131072 | tf_op jit(solution)/shard_map/all_to_all | solution.py:180
  52.0 13.7 %all-gather.1 = bf16[3968,128]{1,0:T(8,128)(2,1)S(1)} all-gather(bf16[992,128]{1,0:T(8,128)(2,1)S(1)} %get-tuple-element.6), channel_id=3, replica_groups=mesh['x'=4,'zh'=2,'c'=2,'y'=8,'zl'=4] {'x'}, dimensions={0}, use_global_device_ids=true | all-gather | bytes 1269760 | tf_op jit(solution)/shard_map/all_gather | solution.py:181
  65.7 0.0 all-to-all-done.1
  65.7 3.8 %collective-permute-start.2 = (bf16[4,992,128]{2,1,0:T(8,128)(2,1)S(1)}, bf16[4,992,128]{2,1,0:T(8,128)(2,1)S(1)}, u32[]{:S(2)}, u32[]{:S(2)}) collective-permute-start(bf16[4,992,128]{2,1,0:T(8,128)(2,1)S(1)} %bitcast.6), channel_id=1, source_target_pairs={{0,32},{32,0},{1,33},{33,1},{2,34},{34,2},{3,35},{35,3},{4,36},{36... | collective-permute-start | bytes 3047432 | tf_op jit(solution)/shard_map/ppermute | solution.py:182
  69.6 0.1 pack.1.p0
  69.7 1.9 %collective-permute-start.1 = (f32[136,128]{1,0:T(8,128)S(1)}, f32[136,128]{1,0:T(8,128)S(1)}, u32[]{:S(2)}, u32[]{:S(2)}) collective-permute-start(f32[136,128]{1,0:T(8,128)S(1)} %pack.1.p0), channel_id=1, source_target_pairs={{0,32},{32,0},{1,33},{33,1},{2,34},{34,2},{3,35},{35,3},{4,36},{36... | collective-permute-start | bytes 208904 | tf_op jit(solution)/shard_map/ppermute | solution.py:188
  71.6 1.2 %collective-permute-done.1.p1 = f32[136,128]{1,0:T(8,128)S(1)} collective-permute-done((f32[136,128]{1,0:T(8,128)S(1)}, f32[136,128]{1,0:T(8,128)S(1)}, u32[]{:S(2)}, u32[]{:S(2)}) %collective-permute-start.1) | collective-permute-done | bytes 69664 | tf_op jit(solution)/shard_map/ppermute | solution.py:188
  72.9 0.0 collective-permute-done.2.s1
  72.9 0.0 copy-done
  72.9 2.3 %final.1 = (bf16[64,8192]{1,0:T(8,128)(2,1)}, f32[64,512]{1,0:T(8,128)}) custom-call(f32[136,128]{1,0:T(8,128)S(1)} %pack.1.p0, f32[136,128]{1,0:T(8,128)S(1)} %collective-permute-done.1.p1, bf16[64,8192]{1,0:T(8,128)(2,1)S(1)} %copy-done, f32[64,512]{1,0:T(8,128)S(1)} %copy-done.1, bf16[4,992,128]{2,1,0:T(8,128)(2,1)S(1)} %bitcast.7, ...), custom_call_target="tpu_custom_call" | custom-call | tf_op jit(solution)/shard_map/final/pallas_call | solution.py:190
Async XLA Ops:
  0.6 10.3 %copy-start.1 = (f32[64,512]{1,0:T(8,128)S(1)}, f32[64,512]{1,0:T(8,128)}, u32[]{:S(2)}) copy-start(f32[64,512]{1,0:T(8,128)} %mom.1) | copy-start | bytes 393220
  2.1 10.3 %collective-permute-start = (bf16[4,528,128]{2,1,0:T(8,128)(2,1)S(1)}, bf16[4,528,128]{2,1,0:T(8,128)(2,1)S(1)}, u32[]{:S(2)}, u32[]{:S(2)}) collective-permute-start(bf16[4,528,128]{2,1,0:T(8,128)(2,1)S(1)} %delta_send.1), channel_id=1, source_target_pairs={{0,32},{32,0},{1,33},{33,1},{2,34},{34,2},{3,35},{35,3},{4,36},{36... | collective-permute-start | bytes 1622024 | tf_op jit(solution)/shard_map/ppermute | solution.py:167
  35.2 37.6 %copy-start = (bf16[64,8192]{1,0:T(8,128)(2,1)S(1)}, bf16[64,8192]{1,0:T(8,128)(2,1)}, u32[]{:S(2)}) copy-start(bf16[64,8192]{1,0:T(8,128)(2,1)} %base.1) | copy-start | bytes 3145732
  35.3 30.5 %all-to-all-start.1 = ((f32[128,1,2]{2,1,0:T(1,128)}), f32[128,1,2]{2,1,0:T(1,128)S(1)}, u32[]{:S(2)}, u32[]{:S(2)}) async-start(f32[128,1,2]{2,1,0:T(1,128)} %bitcast.2), calls=%async_computation.1 | async-start | bytes 131072 | tf_op jit(solution)/shard_map/all_to_all | solution.py:180
  65.7 7.1 %collective-permute-start.2 = (bf16[4,992,128]{2,1,0:T(8,128)(2,1)S(1)}, bf16[4,992,128]{2,1,0:T(8,128)(2,1)S(1)}, u32[]{:S(2)}, u32[]{:S(2)}) collective-permute-start(bf16[4,992,128]{2,1,0:T(8,128)(2,1)S(1)} %bitcast.6), channel_id=1, source_target_pairs={{0,32},{32,0},{1,33},{33,1},{2,34},{34,2},{3,35},{35,3},{4,36},{36... | collective-permute-start | bytes 3047432 | tf_op jit(solution)/shard_map/ppermute | solution.py:182
  69.7 3.2 %collective-permute-start.1 = (f32[136,128]{1,0:T(8,128)S(1)}, f32[136,128]{1,0:T(8,128)S(1)}, u32[]{:S(2)}, u32[]{:S(2)}) collective-permute-start(f32[136,128]{1,0:T(8,128)S(1)} %pack.1.p0), channel_id=1, source_target_pairs={{0,32},{32,0},{1,33},{33,1},{2,34},{34,2},{3,35},{35,3},{4,36},{36... | collective-permute-start | bytes 208904 | tf_op jit(solution)/shard_map/ppermute | solution.py:188

commit v3 on v2

v3 whole, which is shorter than its diff:
```python
import jax
import jax.numpy as jnp
from jax import lax
from jax.experimental import pallas as pl
from jax.experimental.pallas import tpu as pltpu
from jax.sharding import Mesh, PartitionSpec as P

NX, NZ, NC, NY, NL = 4, 2, 2, 8, 4
AXES = ("x", "zh", "c", "y", "zl")
REPLICA = ("x", "zh", "c")
FSDP = ("y", "zl")
REPLICAS = NX * NZ * NC
ROWS = 64
OWN = 512
LANES = 128
TILES = OWN // LANES
SUMS = NZ * TILES * ROWS
MOM = TILES * ROWS
REST = 16
MOST = MOM - REST
QUAD = SUMS + NX * REST
GATHER = SUMS + NZ * MOST
TILE = 16
RESTS = NX * GATHER
SCALARS = RESTS + NZ * NX * REST
PACK = SCALARS + 3 * TILE
F32, BF16 = jnp.float32, jnp.bfloat16
VMEM = pl.BlockSpec(memory_space=pltpu.VMEM)
HBM = pl.BlockSpec(memory_space=pl.ANY)
SMALL = pltpu.CompilerParams(vmem_limit_bytes=4 * 1024 * 1024)


def near(x):
    return pltpu.with_memory_space_constraint(x, pltpu.VMEM)


def far(x):
    return pltpu.with_memory_space_constraint(x, pltpu.HBM)


def flat(tile):
    return slice(tile * ROWS, (tile + 1) * ROWS)


def block_cols(x, h, core, t):
    return pl.ds(pl.multiple_of(((x * NZ + h) * NC + core) * OWN + t * LANES, LANES), LANES)


def fetch_kernel(local_ref, base_ref, mom_ref, local_out, base_out, rest_out, sems):
    core = lax.axis_index("c")
    copies = [
        pltpu.make_async_copy(
            mom_ref.at[ROWS - REST:, OWN - LANES:], rest_out, sems.at[2 * NX * NZ]
        )
    ]
    for x in range(NX):
        for h in range(NZ):
            start = ((x * NZ + h) * NC + core) * OWN
            cols = pl.ds(pl.multiple_of(start, OWN), OWN)
            to = slice(h * OWN, (h + 1) * OWN)
            at = 2 * (x * NZ + h)
            copies.append(pltpu.make_async_copy(local_ref.at[0, :, cols], local_out.at[x, :, to], sems.at[at]))
            copies.append(pltpu.make_async_copy(base_ref.at[:, cols], base_out.at[x, :, to], sems.at[at + 1]))
    for copy in copies:
        copy.start()
    for copy in copies:
        copy.wait()


def fetch(local, base, momentum):
    half = pltpu.VMEM((NX, ROWS, NZ * OWN), BF16)
    return pl.pallas_call(
        fetch_kernel,
        in_specs=[HBM] * 3,
        out_specs=[VMEM] * 3,
        out_shape=[half, half, pltpu.VMEM((REST, LANES), F32)],
        scratch_shapes=[pltpu.SemaphoreType.DMA((2 * NX * NZ + 1,))],
        cost_estimate=pl.CostEstimate(flops=0, bytes_accessed=2**22, transcendentals=0),
        compiler_params=SMALL,
        name="fetch",
    )(far(local), far(base), far(momentum))


def pair_kernel(local_ref, base_ref, rest_ref, got_ref, out_ref):
    core = lax.axis_index("c")
    for x in range(NX):
        for h in range(NZ):
            for t in range(TILES):
                cols = slice(h * OWN + t * LANES, h * OWN + (t + 1) * LANES)
                base = base_ref[x, :, cols].astype(F32)
                got = got_ref[0, :, block_cols(x, h, core, t)].astype(F32)
                pair = (local_ref[x, :, cols].astype(F32) - base) + (got - base)
                out_ref[x, flat(h * TILES + t), :] = pair.astype(BF16)
        out_ref[x, SUMS:, :] = rest_ref[...].astype(BF16)


def quad_kernel(parts_ref, out_ref):
    for t in range(NZ * TILES):
        total = parts_ref[0, flat(t), :].astype(F32)
        for k in range(1, NX):
            total = total + parts_ref[k, flat(t), :].astype(F32)
        out_ref[flat(t), :] = total.astype(BF16)
    for k in range(NX):
        at = SUMS + k * REST
        out_ref[at:at + REST, :] = parts_ref[k, SUMS:, :]


def total_kernel(both_ref, mine_ref, theirs_ref, out_ref, squares_ref):
    acc = jnp.zeros((ROWS, LANES), F32)
    for t in range(NZ * TILES):
        total = both_ref[0, flat(t), :].astype(F32) + both_ref[1, flat(t), :].astype(F32)
        total = total.astype(BF16)
        out_ref[flat(t), :] = total
        acc = acc + total.astype(F32) * total.astype(F32)
    half = lax.axis_index("zh")
    for t in range(TILES):
        rows = ROWS - REST if t == TILES - 1 else ROWS
        mine = mine_ref[:rows, t * LANES:(t + 1) * LANES]
        theirs = theirs_ref[:rows, t * LANES:(t + 1) * LANES]
        for h in range(NZ):
            at = SUMS + h * MOST + t * ROWS
            out_ref[at:at + rows, :] = jnp.where(half == h, mine, theirs).astype(BF16)
    squares_ref[...] = jnp.broadcast_to(jnp.sum(acc), squares_ref.shape)


def pack_kernel(shares_ref, own_ref, both_ref, out_ref):
    for x in range(NX):
        out_ref[x * GATHER:(x + 1) * GATHER, :] = own_ref[x]
    for h in range(NZ):
        at = RESTS + h * NX * REST
        out_ref[at:at + NX * REST, :] = both_ref[h, SUMS:, :]
    left = jnp.broadcast_to(jnp.sum(shares_ref[:, 0:1]), (TILE, LANES))
    for k in range(3):
        part = left.astype(BF16)
        out_ref[SCALARS + k * TILE:SCALARS + (k + 1) * TILE, :] = part
        left = left - part.astype(F32)


def final_kernel(entries, base_ref, mom_ref, mine_ref, theirs_ref, new_ref, newmom_ref, buf, sems):
    core = lax.axis_index("c")
    squares = 0.0
    for pack in (mine_ref, theirs_ref):
        parts = [jnp.sum(pack[at:at + TILE, :][0:1, 0:1].astype(F32)) for at in range(SCALARS, PACK, TILE)]
        squares = squares + ((parts[2] + parts[1]) + parts[0])
    mean = squares / (REPLICAS * REPLICAS) / entries
    factor = jnp.minimum(1.0, 0.04 / jnp.sqrt(mean + 1e-06)) / REPLICAS
    sum_weight = (0.7 * 1.9) * factor

    def weights(rows, cols, total, mom):
        update = sum_weight * total.astype(F32) + (0.7 * 0.81) * mom.astype(F32)
        buf[rows, cols] = (base_ref[rows, cols].astype(F32) - update).astype(BF16)

    copies = []
    for x in range(NX):
        for which, pack in enumerate((mine_ref, theirs_ref)):
            owner = core if which == 0 else 1 - core
            for h in range(NZ):
                for t in range(TILES):
                    cols = block_cols(x, h, owner, t)
                    at = x * GATHER + (h * TILES + t) * ROWS
                    mom_at = x * GATHER + SUMS + h * MOST + t * ROWS
                    rows = ROWS - REST if t == TILES - 1 else ROWS
                    weights(slice(0, rows), cols, pack[at:at + rows, :], pack[mom_at:mom_at + rows, :])
                    if rows < ROWS:
                        rest_at = RESTS + (h * NX + x) * REST
                        weights(slice(rows, ROWS), cols, pack[at + rows:at + ROWS, :], pack[rest_at:rest_at + REST, :])
        cols = slice(x * NZ * NC * OWN, (x + 1) * NZ * NC * OWN)
        copies.append(pltpu.make_async_copy(buf.at[:, cols], new_ref.at[:, cols], sems.at[x]))
        copies[-1].start()
    for t in range(TILES):
        at = lax.axis_index("x") * GATHER + (lax.axis_index("zh") * TILES + t) * ROWS
        total = mine_ref[pl.ds(pl.multiple_of(at, TILE), ROWS), :].astype(F32)
        cols = slice(t * LANES, (t + 1) * LANES)
        newmom_ref[:, cols] = 0.9 * mom_ref[:, cols] + factor * total
    for copy in copies:
        copy.wait()


def per_device(local_weights, global_weights, momentum):
    rows, width = global_weights.shape
    swap = [(0, 1), (1, 0)]
    theirs = lax.ppermute(momentum, "zh", swap)
    got = lax.ppermute(local_weights, "c", swap)
    mine, base, rest = fetch(local_weights, global_weights, momentum)
    pair = pl.pallas_call(
        pair_kernel, in_specs=[VMEM] * 4, out_specs=VMEM,
        out_shape=pltpu.VMEM((NX, SUMS + REST, LANES), BF16),
        compiler_params=SMALL, name="pair",
    )(near(mine), near(base), near(rest), near(got))
    parts = lax.all_to_all(pair, "x", 0, 0, tiled=True)
    quad = pl.pallas_call(
        quad_kernel, in_specs=[VMEM], out_specs=VMEM, out_shape=pltpu.VMEM((QUAD, LANES), BF16),
        compiler_params=SMALL, name="quad",
    )(near(parts))
    both = lax.all_gather(quad, "zh", axis=0)
    group = NX * NY * NL
    total, squares = pl.pallas_call(
        total_kernel, in_specs=[VMEM] * 3, out_specs=[VMEM, VMEM],
        out_shape=[pltpu.VMEM((GATHER, LANES), BF16), pltpu.VMEM((group, 2), F32)],
        compiler_params=SMALL, name="total",
    )(near(both), near(momentum), near(theirs))
    shares = lax.all_to_all(squares, ("x", "y", "zl"), 0, 0, tiled=True)
    own = lax.all_gather(total, "x", axis=0)
    pack = pl.pallas_call(
        pack_kernel, in_specs=[VMEM] * 3, out_specs=VMEM, out_shape=pltpu.VMEM((PACK, LANES), BF16),
        compiler_params=SMALL, name="pack",
    )(near(shares), near(own), near(both))
    other = lax.ppermute(pack, "c", swap)
    entries = rows * width * NY * NL
    return pl.pallas_call(
        lambda *refs: final_kernel(entries, *refs),
        in_specs=[VMEM] * 4, out_specs=[HBM, VMEM],
        out_shape=[jax.ShapeDtypeStruct((rows, width), BF16), jax.ShapeDtypeStruct(momentum.shape, F32)],
        scratch_shapes=[pltpu.VMEM((rows, width), BF16), pltpu.SemaphoreType.DMA((NX,))],
        compiler_params=SMALL, name="final",
    )(near(global_weights), near(momentum), near(pack), near(other))


def solution(mesh):
    fine = Mesh(mesh.devices.reshape(NX, NZ, NC, NY, NL), AXES)
    in_specs = (P(REPLICA, FSDP, None), P(FSDP, None), P(FSDP, REPLICA))
    out_specs = (P(FSDP, None), P(FSDP, REPLICA))
    return jax.shard_map(
        per_device, mesh=fine, in_specs=in_specs, out_specs=out_specs, check_vma=False
    )
```

time: 75.5 us -> 73.5 us (0.974)
  blocking collectives: 35.5 us -> 25.2 us
  waiting for transfers between devices: 1.34 us -> 6.89 us
  starting transfers between devices: 31.3 us -> 34.7 us
    all_to_all x1 -> x0, blocking collectives: 11.8 us -> none  [per_device(): parts = lax.all_to_all(pair, 'x', 0, 0, tiled=True)]
    all_to_all x1, starting transfers between devices: 16.8 us -> 11.3 us  [per_device(): shares = lax.all_to_all(squares, ('x', 'y', 'zl'), 0, 0, tiled=True)]
    ppermute x3, starting transfers between devices: 14.5 us -> 19.8 us  [the longest x1 8.79 us: per_device(): got = lax.ppermute(local_weights, 'c', swap)]
    all_to_all x0 -> x1, starting transfers between devices: none -> 3.6 us  [per_device(): parts = lax.all_to_all(pair, 'x', 0, 0, tiled=True)]
    all_to_all x0 -> x1, waiting for transfers between devices: none -> 3.55 us  [per_device(): parts = lax.all_to_all(pair, 'x', 0, 0, tiled=True)]
    all_gather x1, blocking collectives: 10 us -> 12.1 us  [per_device(): both = lax.all_gather(quad, 'zh', axis=0)]
    ppermute x3, waiting for transfers between devices: 1.34 us -> 3.34 us  [the longest x1 2.28 us: per_device(): other = lax.ppermute(pack, 'c', swap)]
  transfers between devices with their start and end apart: 4 -> 5, of which waited for: 2 -> 3; matrix products, arithmetic and copies ran while one was open for 0% -> 0% of each run, Pallas kernels for 2% -> 2%
where the time goes in v3:
time: 73.5 us; the launch traced here: 73.1 us
  starting transfers between devices  34.7 us (47%)
  blocking collectives  25.2 us (34%)
  waiting for transfers between devices  6.89 us (9%)
  Pallas kernels  5.59 us (8%)
    all_gather x1, blocking collectives, per_device(): own = lax.all_gather(total, 'x', axis=0)  13.1 us
    all_gather x1, blocking collectives, per_device(): both = lax.all_gather(quad, 'zh', axis=0)  12.1 us
    all_to_all x1, starting transfers between devices, per_device(): shares = lax.all_to_all(squares, ('x', 'y', 'zl'), 0, 0, tiled=True)  11.3 us
    ppermute x1, starting transfers between devices, per_device(): got = lax.ppermute(local_weights, 'c', swap)  8.79 us
    ppermute x1, starting transfers between devices, per_device(): theirs = lax.ppermute(momentum, 'zh', swap)  5.78 us
    ppermute x1, starting transfers between devices, per_device(): other = lax.ppermute(pack, 'c', swap)  5.22 us
    all_to_all x1, starting transfers between devices, per_device(): parts = lax.all_to_all(pair, 'x', 0, 0, tiled=True)  3.6 us
    all_to_all x1, waiting for transfers between devices, per_device(): parts = lax.all_to_all(pair, 'x', 0, 0, tiled=True)  3.55 us
  transfers between devices with their start and end apart: 5, of which 3 were waited for; matrix products, arithmetic and copies ran while one was open for 0% of the time, Pallas kernels for 2%

profile of v3, /device:TPU:1, one launch (start us, length us, event | category | flops | bytes accessed | tf_op | source)
XLA Modules:
  0.0 73.1 jit_solution(16368451631454323712)
XLA Ops:
  0.6 8.8 %collective-permute-start = (bf16[1,64,8192]{2,1,0:T(8,128)(2,1)}, bf16[1,64,8192]{2,1,0:T(8,128)(2,1)S(1)}, u32[]{:S(2)}, u32[]{:S(2)}) collective-permute-start(bf16[1,64,8192]{2,1,0:T(8,128)(2,1)} %local_ref.1), channel_id=1, source_target_pairs={{0,32},{32,0},{1,33},{33,1},{2,34},{34,2},{3,35},{35,3},{4,36},{36... | collective-permute-start | bytes 3145736 | tf_op jit(solution)/shard_map/ppermute | solution.py:183
  9.4 1.4 %fetch.1 = (bf16[4,64,1024]{2,1,0:T(8,128)(2,1)S(1)}, bf16[4,64,1024]{2,1,0:T(8,128)(2,1)S(1)}, f32[16,128]{1,0:T(8,128)S(1)}) custom-call(bf16[1,64,8192]{2,1,0:T(8,128)(2,1)} %local_ref.1, bf16[64,8192]{1,0:T(8,128)(2,1)} %refs_0_.1, f32[64,512]{1,0:T(8,128)} %refs_1_.1), custom_call_target="tpu_custom_call" | custom-call | bytes 4194304 | tf_op jit(solution)/shard_map/fetch/pallas_call | solution.py:72
  10.8 1.1 %collective-permute-done.got_ref = bf16[1,64,8192]{2,1,0:T(8,128)(2,1)S(1)} collective-permute-done((bf16[1,64,8192]{2,1,0:T(8,128)(2,1)}, bf16[1,64,8192]{2,1,0:T(8,128)(2,1)S(1)}, u32[]{:S(2)}, u32[]{:S(2)}) %collective-permute-start) | collective-permute-done | bytes 1048608 | tf_op jit(solution)/shard_map/ppermute | solution.py:183
  11.9 1.0 %pair.1 = bf16[4,528,128]{2,1,0:T(8,128)(2,1)} custom-call(bf16[4,64,1024]{2,1,0:T(8,128)(2,1)S(1)} %get-tuple-element.7.local_ref, bf16[4,64,1024]{2,1,0:T(8,128)(2,1)S(1)} %get-tuple-element.8.base_ref, f32[16,128]{1,0:T(8,128)S(1)} %get-tuple-element.9.rest_ref, bf16[1,64,8192]{2,1,0:T(8,128)(2,1)S(1)} %collective-permute-done.got_ref), custom_call_target="tpu_custom_call" | custom-call | tf_op jit(solution)/shard_map/pair/pallas_call | solution.py:185
  12.9 0.0 copy-start.1
  12.9 3.6 %all-to-all-start = ((bf16[4,528,128]{2,1,0:T(8,128)(2,1)}), bf16[4,528,128]{2,1,0:T(8,128)(2,1)S(1)}, u32[]{:S(2)}, u32[]{:S(2)}) async-start(bf16[4,528,128]{2,1,0:T(8,128)(2,1)} %pair.1), calls=%async_computation | async-start | bytes 1081344 | tf_op jit(solution)/shard_map/all_to_all | solution.py:190
  16.6 0.0 copy-done.1
  16.6 5.8 %collective-permute-start.1 = (f32[64,512]{1,0:T(8,128)S(1)}, f32[64,512]{1,0:T(8,128)S(1)}, u32[]{:S(2)}, u32[]{:S(2)}) collective-permute-start(f32[64,512]{1,0:T(8,128)S(1)} %copy-done.1), channel_id=1, source_target_pairs={{0,64},{64,0},{1,65},{65,1},{2,66},{66,2},{3,67},{67,3},{4,68},{68... | collective-permute-start | bytes 393224 | tf_op jit(solution)/shard_map/ppermute | solution.py:182
  22.4 3.5 %all-to-all-done.parts_ref = bf16[4,528,128]{2,1,0:T(8,128)(2,1)S(1)} async-done(((bf16[4,528,128]{2,1,0:T(8,128)(2,1)}), bf16[4,528,128]{2,1,0:T(8,128)(2,1)S(1)}, u32[]{:S(2)}, u32[]{:S(2)}) %all-to-all-start) | async-done | bytes 540704 | tf_op jit(solution)/shard_map/all_to_all | solution.py:190
  25.9 0.1 quad.1
  26.0 12.1 %all-gather = bf16[1152,128]{1,0:T(8,128)(2,1)S(1)} all-gather(bf16[576,128]{1,0:T(8,128)(2,1)S(1)} %quad.1), channel_id=2, replica_groups=mesh['x'=4,'zh'=2,'c'=2,'y'=8,'zl'=4] {'zh'}, dimensions={0}, use_global_device_ids=true | all-gather | bytes 442368 | tf_op jit(solution)/shard_map/all_gather | solution.py:195
  38.1 0.0 collective-permute-done.1.theirs_ref
  38.1 0.8 %total.1 = (bf16[992,128]{1,0:T(8,128)(2,1)S(1)}, f32[128,2]{1,0:T(8,128)}) custom-call(bf16[2,576,128]{2,1,0:T(8,128)(2,1)S(1)} %bitcast.7, f32[64,512]{1,0:T(8,128)S(1)} %copy-done.1, f32[64,512]{1,0:T(8,128)S(1)} %collective-permute-done.1.theirs_ref), custom_call_target="tpu_custom_call" | custom-call | tf_op jit(solution)/shard_map/total/pallas_call | solution.py:197
  38.9 11.3 %all-to-all-start.1 = ((f32[128,1,2]{2,1,0:T(1,128)}), f32[128,1,2]{2,1,0:T(1,128)S(1)}, u32[]{:S(2)}, u32[]{:S(2)}) async-start(f32[128,1,2]{2,1,0:T(1,128)} %bitcast.2), calls=%async_computation.1 | async-start | bytes 131072 | tf_op jit(solution)/shard_map/all_to_all | solution.py:202
  50.3 13.1 %all-gather.1 = bf16[3968,128]{1,0:T(8,128)(2,1)S(1)} all-gather(bf16[992,128]{1,0:T(8,128)(2,1)S(1)} %get-tuple-element.11), channel_id=3, replica_groups=mesh['x'=4,'zh'=2,'c'=2,'y'=8,'zl'=4] {'x'}, dimensions={0}, use_global_device_ids=true | all-gather | bytes 1269760 | tf_op jit(solution)/shard_map/all_gather | solution.py:203
  63.4 0.0 all-to-all-done.1
  63.4 0.0 copy-start
  63.4 0.2 pack.1.refs_2_
  63.6 5.2 %collective-permute-start.2 = (bf16[4144,128]{1,0:T(8,128)(2,1)S(1)}, bf16[4144,128]{1,0:T(8,128)(2,1)S(1)}, u32[]{:S(2)}, u32[]{:S(2)}) collective-permute-start(bf16[4144,128]{1,0:T(8,128)(2,1)S(1)} %pack.1.refs_2_), channel_id=1, source_target_pairs={{0,32},{32,0},{1,33},{33,1},{2,34},{34,2},{3,35},{35,3},{4,36},{36... | collective-permute-start | bytes 3182600 | tf_op jit(solution)/shard_map/ppermute | solution.py:208
  68.8 2.3 %collective-permute-done.2.refs_3_ = bf16[4144,128]{1,0:T(8,128)(2,1)S(1)} collective-permute-done((bf16[4144,128]{1,0:T(8,128)(2,1)S(1)}, bf16[4144,128]{1,0:T(8,128)(2,1)S(1)}, u32[]{:S(2)}, u32[]{:S(2)}) %collective-permute-start.2) | collective-permute-done | bytes 1060896 | tf_op jit(solution)/shard_map/ppermute | solution.py:208
  71.1 0.0 copy-done
  71.1 2.1 %final.1 = (bf16[64,8192]{1,0:T(8,128)(2,1)}, f32[64,512]{1,0:T(8,128)}) custom-call(bf16[64,8192]{1,0:T(8,128)(2,1)S(1)} %copy-done, f32[64,512]{1,0:T(8,128)S(1)} %copy-done.1, bf16[4144,128]{1,0:T(8,128)(2,1)S(1)} %pack.1.refs_2_, bf16[4144,128]{1,0:T(8,128)(2,1)S(1)} %collective-permute-done.2.refs_3_), custom_call_target="tpu_custom_call" | custom-call | tf_op jit(solution)/shard_map/final/pallas_call | solution.py:210
Async XLA Ops:
  0.6 11.3 %collective-permute-start = (bf16[1,64,8192]{2,1,0:T(8,128)(2,1)}, bf16[1,64,8192]{2,1,0:T(8,128)(2,1)S(1)}, u32[]{:S(2)}, u32[]{:S(2)}) collective-permute-start(bf16[1,64,8192]{2,1,0:T(8,128)(2,1)} %local_ref.1), channel_id=1, source_target_pairs={{0,32},{32,0},{1,33},{33,1},{2,34},{34,2},{3,35},{35,3},{4,36},{36... | collective-permute-start | bytes 3145736 | tf_op jit(solution)/shard_map/ppermute | solution.py:183
  12.9 3.6 %copy-start.1 = (f32[64,512]{1,0:T(8,128)S(1)}, f32[64,512]{1,0:T(8,128)}, u32[]{:S(2)}) copy-start(f32[64,512]{1,0:T(8,128)} %refs_1_.1) | copy-start | bytes 393220
  12.9 13.0 %all-to-all-start = ((bf16[4,528,128]{2,1,0:T(8,128)(2,1)}), bf16[4,528,128]{2,1,0:T(8,128)(2,1)S(1)}, u32[]{:S(2)}, u32[]{:S(2)}) async-start(bf16[4,528,128]{2,1,0:T(8,128)(2,1)} %pair.1), calls=%async_computation | async-start | bytes 1081344 | tf_op jit(solution)/shard_map/all_to_all | solution.py:190
  16.6 21.6 %collective-permute-start.1 = (f32[64,512]{1,0:T(8,128)S(1)}, f32[64,512]{1,0:T(8,128)S(1)}, u32[]{:S(2)}, u32[]{:S(2)}) collective-permute-start(f32[64,512]{1,0:T(8,128)S(1)} %copy-done.1), channel_id=1, source_target_pairs={{0,64},{64,0},{1,65},{65,1},{2,66},{66,2},{3,67},{67,3},{4,68},{68... | collective-permute-start | bytes 393224 | tf_op jit(solution)/shard_map/ppermute | solution.py:182
  38.9 24.4 %all-to-all-start.1 = ((f32[128,1,2]{2,1,0:T(1,128)}), f32[128,1,2]{2,1,0:T(1,128)S(1)}, u32[]{:S(2)}, u32[]{:S(2)}) async-start(f32[128,1,2]{2,1,0:T(1,128)} %bitcast.2), calls=%async_computation.1 | async-start | bytes 131072 | tf_op jit(solution)/shard_map/all_to_all | solution.py:202
  63.4 7.7 %copy-start = (bf16[64,8192]{1,0:T(8,128)(2,1)S(1)}, bf16[64,8192]{1,0:T(8,128)(2,1)}, u32[]{:S(2)}) copy-start(bf16[64,8192]{1,0:T(8,128)(2,1)} %refs_0_.1) | copy-start | bytes 3145732
  63.6 7.5 %collective-permute-start.2 = (bf16[4144,128]{1,0:T(8,128)(2,1)S(1)}, bf16[4144,128]{1,0:T(8,128)(2,1)S(1)}, u32[]{:S(2)}, u32[]{:S(2)}) collective-permute-start(bf16[4144,128]{1,0:T(8,128)(2,1)S(1)} %pack.1.refs_2_), channel_id=1, source_target_pairs={{0,32},{32,0},{1,33},{33,1},{2,34},{34,2},{3,35},{35,3},{4,36},{36... | collective-permute-start | bytes 3182600 | tf_op jit(solution)/shard_map/ppermute | solution.py:208

commit v4 on v3

--- a/solution.py
+++ b/solution.py
@@ -115,11 +115,11 @@
     half = lax.axis_index("zh")
     for t in range(TILES):
         rows = ROWS - REST if t == TILES - 1 else ROWS
-        mine = mine_ref[:rows, t * LANES:(t + 1) * LANES]
+        mine = mine_ref[:rows, t * LANES:(t + 1) * LANES].astype(BF16)
         theirs = theirs_ref[:rows, t * LANES:(t + 1) * LANES]
         for h in range(NZ):
             at = SUMS + h * MOST + t * ROWS
-            out_ref[at:at + rows, :] = jnp.where(half == h, mine, theirs).astype(BF16)
+            out_ref[at:at + rows, :] = jnp.where(half == h, mine, theirs)
     squares_ref[...] = jnp.broadcast_to(jnp.sum(acc), squares_ref.shape)
 
 
@@ -152,9 +152,9 @@
 
     copies = []
     for x in range(NX):
-        for which, pack in enumerate((mine_ref, theirs_ref)):
-            owner = core if which == 0 else 1 - core
-            for h in range(NZ):
+        for h in range(NZ):
+            for which, pack in enumerate((mine_ref, theirs_ref)):
+                owner = core if which == 0 else 1 - core
                 for t in range(TILES):
                     cols = block_cols(x, h, owner, t)
                     at = x * GATHER + (h * TILES + t) * ROWS
@@ -164,9 +164,10 @@
                     if rows < ROWS:
                         rest_at = RESTS + (h * NX + x) * REST
                         weights(slice(rows, ROWS), cols, pack[at + rows:at + ROWS, :], pack[rest_at:rest_at + REST, :])
-        cols = slice(x * NZ * NC * OWN, (x + 1) * NZ * NC * OWN)
-        copies.append(pltpu.make_async_copy(buf.at[:, cols], new_ref.at[:, cols], sems.at[x]))
-        copies[-1].start()
+            at = (x * NZ + h) * NC * OWN
+            cols = slice(at, at + NC * OWN)
+            copies.append(pltpu.make_async_copy(buf.at[:, cols], new_ref.at[:, cols], sems.at[x * NZ + h]))
+            copies[-1].start()
     for t in range(TILES):
         at = lax.axis_index("x") * GATHER + (lax.axis_index("zh") * TILES + t) * ROWS
         total = mine_ref[pl.ds(pl.multiple_of(at, TILE), ROWS), :].astype(F32)
@@ -179,7 +180,7 @@
 def per_device(local_weights, global_weights, momentum):
     rows, width = global_weights.shape
     swap = [(0, 1), (1, 0)]
-    theirs = lax.ppermute(momentum, "zh", swap)
+    theirs = lax.ppermute(momentum.astype(BF16), "zh", swap)
     got = lax.ppermute(local_weights, "c", swap)
     mine, base, rest = fetch(local_weights, global_weights, momentum)
     pair = pl.pallas_call(
@@ -211,7 +212,7 @@
         lambda *refs: final_kernel(entries, *refs),
         in_specs=[VMEM] * 4, out_specs=[HBM, VMEM],
         out_shape=[jax.ShapeDtypeStruct((rows, width), BF16), jax.ShapeDtypeStruct(momentum.shape, F32)],
-        scratch_shapes=[pltpu.VMEM((rows, width), BF16), pltpu.SemaphoreType.DMA((NX,))],
+        scratch_shapes=[pltpu.VMEM((rows, width), BF16), pltpu.SemaphoreType.DMA((NX * NZ,))],
         compiler_params=SMALL, name="final",
     )(near(global_weights), near(momentum), near(pack), near(other))
 

time: 73.5 us -> 72.8 us (level)
  blocking collectives: 25.2 us -> 21.9 us
  starting transfers between devices: 34.7 us -> 37.3 us
    all_gather x1, blocking collectives: 12.1 us -> 8.76 us  [per_device(): both = lax.all_gather(quad, 'zh', axis=0)]
    all_to_all x1, starting transfers between devices: 11.3 us -> 13.8 us  [per_device(): shares = lax.all_to_all(squares, ('x', 'y', 'zl'), 0, 0, tiled=True)]
where the time goes in v4:
time: 72.8 us; the launch traced here: 72.4 us
  starting transfers between devices  37.3 us (51%)
  blocking collectives  21.9 us (30%)
  waiting for transfers between devices  6.87 us (9%)
  Pallas kernels  5.59 us (8%)
    all_to_all x1, starting transfers between devices, per_device(): shares = lax.all_to_all(squares, ('x', 'y', 'zl'), 0, 0, tiled=True)  13.8 us
    all_gather x1, blocking collectives, per_device(): own = lax.all_gather(total, 'x', axis=0)  13.2 us
    ppermute x1, starting transfers between devices, per_device(): got = lax.ppermute(local_weights, 'c', swap)  8.79 us
    all_gather x1, blocking collectives, per_device(): both = lax.all_gather(quad, 'zh', axis=0)  8.76 us
    ppermute x1, starting transfers between devices, per_device(): theirs = lax.ppermute(momentum.astype(BF16), 'zh', swap)  5.78 us
    ppermute x1, starting transfers between devices, per_device(): other = lax.ppermute(pack, 'c', swap)  5.35 us
    all_to_all x1, starting transfers between devices, per_device(): parts = lax.all_to_all(pair, 'x', 0, 0, tiled=True)  3.6 us
    all_to_all x1, waiting for transfers between devices, per_device(): parts = lax.all_to_all(pair, 'x', 0, 0, tiled=True)  3.52 us
  transfers between devices with their start and end apart: 5, of which 3 were waited for; matrix products, arithmetic and copies ran while one was open for 0% of the time, Pallas kernels for 2%

profile of v4, /device:TPU:1, one launch (start us, length us, event | category | flops | bytes accessed | tf_op | source)
XLA Modules:
  0.0 72.4 jit_solution(13278292451742234153)
XLA Ops:
  0.6 8.8 %collective-permute-start = (bf16[1,64,8192]{2,1,0:T(8,128)(2,1)}, bf16[1,64,8192]{2,1,0:T(8,128)(2,1)S(1)}, u32[]{:S(2)}, u32[]{:S(2)}) collective-permute-start(bf16[1,64,8192]{2,1,0:T(8,128)(2,1)} %local_ref.1), channel_id=1, source_target_pairs={{0,32},{32,0},{1,33},{33,1},{2,34},{34,2},{3,35},{35,3},{4,36},{36... | collective-permute-start | bytes 3145736 | tf_op jit(solution)/shard_map/ppermute | solution.py:184
  9.4 1.4 %fetch.1 = (bf16[4,64,1024]{2,1,0:T(8,128)(2,1)S(1)}, bf16[4,64,1024]{2,1,0:T(8,128)(2,1)S(1)}, f32[16,128]{1,0:T(8,128)S(1)}) custom-call(bf16[1,64,8192]{2,1,0:T(8,128)(2,1)} %local_ref.1, bf16[64,8192]{1,0:T(8,128)(2,1)} %refs_0_.1, f32[64,512]{1,0:T(8,128)} %refs_1_.1), custom_call_target="tpu_custom_call" | custom-call | bytes 4194304 | tf_op jit(solution)/shard_map/fetch/pallas_call | solution.py:72
  10.8 1.1 %collective-permute-done.got_ref = bf16[1,64,8192]{2,1,0:T(8,128)(2,1)S(1)} collective-permute-done((bf16[1,64,8192]{2,1,0:T(8,128)(2,1)}, bf16[1,64,8192]{2,1,0:T(8,128)(2,1)S(1)}, u32[]{:S(2)}, u32[]{:S(2)}) %collective-permute-start) | collective-permute-done | bytes 1048608 | tf_op jit(solution)/shard_map/ppermute | solution.py:184
  11.9 1.0 %pair.1 = bf16[4,528,128]{2,1,0:T(8,128)(2,1)} custom-call(bf16[4,64,1024]{2,1,0:T(8,128)(2,1)S(1)} %get-tuple-element.7.local_ref, bf16[4,64,1024]{2,1,0:T(8,128)(2,1)S(1)} %get-tuple-element.8.base_ref, f32[16,128]{1,0:T(8,128)S(1)} %get-tuple-element.9.rest_ref, bf16[1,64,8192]{2,1,0:T(8,128)(2,1)S(1)} %collective-permute-done.got_ref), custom_call_target="tpu_custom_call" | custom-call | tf_op jit(solution)/shard_map/pair/pallas_call | solution.py:186
  12.9 0.0 copy-start.1
  12.9 3.6 %all-to-all-start = ((bf16[4,528,128]{2,1,0:T(8,128)(2,1)}), bf16[4,528,128]{2,1,0:T(8,128)(2,1)S(1)}, u32[]{:S(2)}, u32[]{:S(2)}) async-start(bf16[4,528,128]{2,1,0:T(8,128)(2,1)} %pair.1), calls=%async_computation | async-start | bytes 1081344 | tf_op jit(solution)/shard_map/all_to_all | solution.py:191
  16.6 0.0 copy-done.1
  16.6 5.8 %collective-permute-start.1 = (bf16[64,512]{1,0:T(8,128)(2,1)S(1)}, bf16[64,512]{1,0:T(8,128)(2,1)S(1)}, u32[]{:S(2)}, u32[]{:S(2)}) collective-permute-start(bf16[64,512]{1,0:T(8,128)(2,1)S(1)} %convert_element_type.3), channel_id=1, source_target_pairs={{0,64},{64,0},{1,65},{65,1},{2,66},{66,2},{3,67},{67,3},{4,68},{68... | collective-permute-start | bytes 196616 | tf_op jit(solution)/shard_map/ppermute | solution.py:183
  22.4 3.5 %all-to-all-done.parts_ref = bf16[4,528,128]{2,1,0:T(8,128)(2,1)S(1)} async-done(((bf16[4,528,128]{2,1,0:T(8,128)(2,1)}), bf16[4,528,128]{2,1,0:T(8,128)(2,1)S(1)}, u32[]{:S(2)}, u32[]{:S(2)}) %all-to-all-start) | async-done | bytes 540704 | tf_op jit(solution)/shard_map/all_to_all | solution.py:191
  25.9 0.1 quad.1
  26.0 8.8 %all-gather = bf16[1152,128]{1,0:T(8,128)(2,1)S(1)} all-gather(bf16[576,128]{1,0:T(8,128)(2,1)S(1)} %quad.1), channel_id=2, replica_groups=mesh['x'=4,'zh'=2,'c'=2,'y'=8,'zl'=4] {'zh'}, dimensions={0}, use_global_device_ids=true | all-gather | bytes 442368 | tf_op jit(solution)/shard_map/all_gather | solution.py:196
  34.7 0.0 collective-permute-done.1.theirs_ref
  34.7 0.8 %total.1 = (bf16[992,128]{1,0:T(8,128)(2,1)S(1)}, f32[128,2]{1,0:T(8,128)}) custom-call(bf16[2,576,128]{2,1,0:T(8,128)(2,1)S(1)} %bitcast.7, f32[64,512]{1,0:T(8,128)S(1)} %copy-done.1, bf16[64,512]{1,0:T(8,128)(2,1)S(1)} %collective-permute-done.1.theirs_ref), custom_call_target="tpu_custom_call" | custom-call | tf_op jit(solution)/shard_map/total/pallas_call | solution.py:198
  35.5 13.8 %all-to-all-start.1 = ((f32[128,1,2]{2,1,0:T(1,128)}), f32[128,1,2]{2,1,0:T(1,128)S(1)}, u32[]{:S(2)}, u32[]{:S(2)}) async-start(f32[128,1,2]{2,1,0:T(1,128)} %bitcast.2), calls=%async_computation.1 | async-start | bytes 131072 | tf_op jit(solution)/shard_map/all_to_all | solution.py:203
  49.3 13.2 %all-gather.1 = bf16[3968,128]{1,0:T(8,128)(2,1)S(1)} all-gather(bf16[992,128]{1,0:T(8,128)(2,1)S(1)} %get-tuple-element.11), channel_id=3, replica_groups=mesh['x'=4,'zh'=2,'c'=2,'y'=8,'zl'=4] {'x'}, dimensions={0}, use_global_device_ids=true | all-gather | bytes 1269760 | tf_op jit(solution)/shard_map/all_gather | solution.py:204
  62.5 0.0 all-to-all-done.1
  62.5 0.0 copy-start
  62.5 0.2 pack.1.refs_2_
  62.7 5.4 %collective-permute-start.2 = (bf16[4144,128]{1,0:T(8,128)(2,1)S(1)}, bf16[4144,128]{1,0:T(8,128)(2,1)S(1)}, u32[]{:S(2)}, u32[]{:S(2)}) collective-permute-start(bf16[4144,128]{1,0:T(8,128)(2,1)S(1)} %pack.1.refs_2_), channel_id=1, source_target_pairs={{0,32},{32,0},{1,33},{33,1},{2,34},{34,2},{3,35},{35,3},{4,36},{36... | collective-permute-start | bytes 3182600 | tf_op jit(solution)/shard_map/ppermute | solution.py:209
  68.1 2.3 %collective-permute-done.2.refs_3_ = bf16[4144,128]{1,0:T(8,128)(2,1)S(1)} collective-permute-done((bf16[4144,128]{1,0:T(8,128)(2,1)S(1)}, bf16[4144,128]{1,0:T(8,128)(2,1)S(1)}, u32[]{:S(2)}, u32[]{:S(2)}) %collective-permute-start.2) | collective-permute-done | bytes 1060896 | tf_op jit(solution)/shard_map/ppermute | solution.py:209
  70.4 0.0 copy-done
  70.4 2.0 %final.1 = (bf16[64,8192]{1,0:T(8,128)(2,1)}, f32[64,512]{1,0:T(8,128)}) custom-call(bf16[64,8192]{1,0:T(8,128)(2,1)S(1)} %copy-done, f32[64,512]{1,0:T(8,128)S(1)} %copy-done.1, bf16[4144,128]{1,0:T(8,128)(2,1)S(1)} %pack.1.refs_2_, bf16[4144,128]{1,0:T(8,128)(2,1)S(1)} %collective-permute-done.2.refs_3_), custom_call_target="tpu_custom_call" | custom-call | tf_op jit(solution)/shard_map/final/pallas_call | solution.py:211
  (1 shorter events, 0.0 us)
Async XLA Ops:
  0.6 11.3 %collective-permute-start = (bf16[1,64,8192]{2,1,0:T(8,128)(2,1)}, bf16[1,64,8192]{2,1,0:T(8,128)(2,1)S(1)}, u32[]{:S(2)}, u32[]{:S(2)}) collective-permute-start(bf16[1,64,8192]{2,1,0:T(8,128)(2,1)} %local_ref.1), channel_id=1, source_target_pairs={{0,32},{32,0},{1,33},{33,1},{2,34},{34,2},{3,35},{35,3},{4,36},{36... | collective-permute-start | bytes 3145736 | tf_op jit(solution)/shard_map/ppermute | solution.py:184
  12.9 3.6 %copy-start.1 = (f32[64,512]{1,0:T(8,128)S(1)}, f32[64,512]{1,0:T(8,128)}, u32[]{:S(2)}) copy-start(f32[64,512]{1,0:T(8,128)} %refs_1_.1) | copy-start | bytes 393220
  12.9 13.0 %all-to-all-start = ((bf16[4,528,128]{2,1,0:T(8,128)(2,1)}), bf16[4,528,128]{2,1,0:T(8,128)(2,1)S(1)}, u32[]{:S(2)}, u32[]{:S(2)}) async-start(bf16[4,528,128]{2,1,0:T(8,128)(2,1)} %pair.1), calls=%async_computation | async-start | bytes 1081344 | tf_op jit(solution)/shard_map/all_to_all | solution.py:191
  16.6 18.2 %collective-permute-start.1 = (bf16[64,512]{1,0:T(8,128)(2,1)S(1)}, bf16[64,512]{1,0:T(8,128)(2,1)S(1)}, u32[]{:S(2)}, u32[]{:S(2)}) collective-permute-start(bf16[64,512]{1,0:T(8,128)(2,1)S(1)} %convert_element_type.3), channel_id=1, source_target_pairs={{0,64},{64,0},{1,65},{65,1},{2,66},{66,2},{3,67},{67,3},{4,68},{68... | collective-permute-start | bytes 196616 | tf_op jit(solution)/shard_map/ppermute | solution.py:183
  35.5 27.0 %all-to-all-start.1 = ((f32[128,1,2]{2,1,0:T(1,128)}), f32[128,1,2]{2,1,0:T(1,128)S(1)}, u32[]{:S(2)}, u32[]{:S(2)}) async-start(f32[128,1,2]{2,1,0:T(1,128)} %bitcast.2), calls=%async_computation.1 | async-start | bytes 131072 | tf_op jit(solution)/shard_map/all_to_all | solution.py:203
  62.5 7.9 %copy-start = (bf16[64,8192]{1,0:T(8,128)(2,1)S(1)}, bf16[64,8192]{1,0:T(8,128)(2,1)}, u32[]{:S(2)}) copy-start(bf16[64,8192]{1,0:T(8,128)(2,1)} %refs_0_.1) | copy-start | bytes 3145732
  62.7 7.6 %collective-permute-start.2 = (bf16[4144,128]{1,0:T(8,128)(2,1)S(1)}, bf16[4144,128]{1,0:T(8,128)(2,1)S(1)}, u32[]{:S(2)}, u32[]{:S(2)}) collective-permute-start(bf16[4144,128]{1,0:T(8,128)(2,1)S(1)} %pack.1.refs_2_), channel_id=1, source_target_pairs={{0,32},{32,0},{1,33},{33,1},{2,34},{34,2},{3,35},{35,3},{4,36},{36... | collective-permute-start | bytes 3182600 | tf_op jit(solution)/shard_map/ppermute | solution.py:209

commit v5 on v4

--- a/solution.py
+++ b/solution.py
@@ -81,8 +81,9 @@
     )(far(local), far(base), far(momentum))
 
 
-def pair_kernel(local_ref, base_ref, rest_ref, got_ref, out_ref):
+def pair_kernel(local_ref, base_ref, rest_ref, got_ref, out_ref, buf, sems):
     core = lax.axis_index("c")
+    copies = []
     for x in range(NX):
         for h in range(NZ):
             for t in range(TILES):
@@ -90,8 +91,12 @@
                 base = base_ref[x, :, cols].astype(F32)
                 got = got_ref[0, :, block_cols(x, h, core, t)].astype(F32)
                 pair = (local_ref[x, :, cols].astype(F32) - base) + (got - base)
-                out_ref[x, flat(h * TILES + t), :] = pair.astype(BF16)
-        out_ref[x, SUMS:, :] = rest_ref[...].astype(BF16)
+                buf[x, flat(h * TILES + t), :] = pair.astype(BF16)
+        buf[x, SUMS:, :] = rest_ref[...].astype(BF16)
+        copies.append(pltpu.make_async_copy(buf.at[x], out_ref.at[x], sems.at[x]))
+        copies[-1].start()
+    for copy in copies:
+        copy.wait()
 
 
 def quad_kernel(parts_ref, out_ref):
@@ -105,13 +110,16 @@
         out_ref[at:at + REST, :] = parts_ref[k, SUMS:, :]
 
 
-def total_kernel(both_ref, mine_ref, theirs_ref, out_ref, squares_ref):
+def total_kernel(both_ref, mine_ref, theirs_ref, out_ref, squares_ref, buf, sem):
     acc = jnp.zeros((ROWS, LANES), F32)
     for t in range(NZ * TILES):
         total = both_ref[0, flat(t), :].astype(F32) + both_ref[1, flat(t), :].astype(F32)
         total = total.astype(BF16)
         out_ref[flat(t), :] = total
         acc = acc + total.astype(F32) * total.astype(F32)
+    buf[...] = jnp.broadcast_to(jnp.sum(acc), buf.shape)
+    copy = pltpu.make_async_copy(buf, squares_ref, sem)
+    copy.start()
     half = lax.axis_index("zh")
     for t in range(TILES):
         rows = ROWS - REST if t == TILES - 1 else ROWS
@@ -120,7 +128,7 @@
         for h in range(NZ):
             at = SUMS + h * MOST + t * ROWS
             out_ref[at:at + rows, :] = jnp.where(half == h, mine, theirs)
-    squares_ref[...] = jnp.broadcast_to(jnp.sum(acc), squares_ref.shape)
+    copy.wait()
 
 
 def pack_kernel(shares_ref, own_ref, both_ref, out_ref):
@@ -138,16 +146,17 @@
 
 def final_kernel(entries, base_ref, mom_ref, mine_ref, theirs_ref, new_ref, newmom_ref, buf, sems):
     core = lax.axis_index("c")
-    squares = 0.0
+    squares = jnp.zeros((8, LANES), F32)
     for pack in (mine_ref, theirs_ref):
-        parts = [jnp.sum(pack[at:at + TILE, :][0:1, 0:1].astype(F32)) for at in range(SCALARS, PACK, TILE)]
+        parts = [pack[at:at + TILE, :].astype(F32)[:8] for at in range(SCALARS, PACK, TILE)]
         squares = squares + ((parts[2] + parts[1]) + parts[0])
     mean = squares / (REPLICAS * REPLICAS) / entries
     factor = jnp.minimum(1.0, 0.04 / jnp.sqrt(mean + 1e-06)) / REPLICAS
     sum_weight = (0.7 * 1.9) * factor
 
     def weights(rows, cols, total, mom):
-        update = sum_weight * total.astype(F32) + (0.7 * 0.81) * mom.astype(F32)
+        scaled = (total.astype(F32).reshape(-1, 8, LANES) * sum_weight[None]).reshape(-1, LANES)
+        update = scaled + (0.7 * 0.81) * mom.astype(F32)
         buf[rows, cols] = (base_ref[rows, cols].astype(F32) - update).astype(BF16)
 
     copies = []
@@ -172,7 +181,8 @@
         at = lax.axis_index("x") * GATHER + (lax.axis_index("zh") * TILES + t) * ROWS
         total = mine_ref[pl.ds(pl.multiple_of(at, TILE), ROWS), :].astype(F32)
         cols = slice(t * LANES, (t + 1) * LANES)
-        newmom_ref[:, cols] = 0.9 * mom_ref[:, cols] + factor * total
+        scaled = (total.reshape(-1, 8, LANES) * factor[None]).reshape(-1, LANES)
+        newmom_ref[:, cols] = 0.9 * mom_ref[:, cols] + scaled
     for copy in copies:
         copy.wait()
 
@@ -184,8 +194,9 @@
     got = lax.ppermute(local_weights, "c", swap)
     mine, base, rest = fetch(local_weights, global_weights, momentum)
     pair = pl.pallas_call(
-        pair_kernel, in_specs=[VMEM] * 4, out_specs=VMEM,
-        out_shape=pltpu.VMEM((NX, SUMS + REST, LANES), BF16),
+        pair_kernel, in_specs=[VMEM] * 4, out_specs=HBM,
+        out_shape=jax.ShapeDtypeStruct((NX, SUMS + REST, LANES), BF16),
+        scratch_shapes=[pltpu.VMEM((NX, SUMS + REST, LANES), BF16), pltpu.SemaphoreType.DMA((NX,))],
         compiler_params=SMALL, name="pair",
     )(near(mine), near(base), near(rest), near(got))
     parts = lax.all_to_all(pair, "x", 0, 0, tiled=True)
@@ -196,8 +207,9 @@
     both = lax.all_gather(quad, "zh", axis=0)
     group = NX * NY * NL
     total, squares = pl.pallas_call(
-        total_kernel, in_specs=[VMEM] * 3, out_specs=[VMEM, VMEM],
-        out_shape=[pltpu.VMEM((GATHER, LANES), BF16), pltpu.VMEM((group, 2), F32)],
+        total_kernel, in_specs=[VMEM] * 3, out_specs=[VMEM, HBM],
+        out_shape=[pltpu.VMEM((GATHER, LANES), BF16), jax.ShapeDtypeStruct((group, 2), F32)],
+        scratch_shapes=[pltpu.VMEM((group, 2), F32), pltpu.SemaphoreType.DMA],
         compiler_params=SMALL, name="total",
     )(near(both), near(momentum), near(theirs))
     shares = lax.all_to_all(squares, ("x", "y", "zl"), 0, 0, tiled=True)

time: 72.8 us -> 72.7 us (level)
  no operation moved by 1% of the time
where the time goes in v5:
time: 72.7 us; the launch traced here: 72.3 us
  starting transfers between devices  37.3 us (51%)
  blocking collectives  21.9 us (30%)
  waiting for transfers between devices  6.87 us (9%)
  Pallas kernels  5.41 us (7%)
  between operations  0.73 us (1%)
    all_to_all x1, starting transfers between devices, per_device(): shares = lax.all_to_all(squares, ('x', 'y', 'zl'), 0, 0, tiled=True)  13.8 us
    all_gather x1, blocking collectives, per_device(): own = lax.all_gather(total, 'x', axis=0)  13.2 us
    ppermute x1, starting transfers between devices, per_device(): got = lax.ppermute(local_weights, 'c', swap)  8.79 us
    all_gather x1, blocking collectives, per_device(): both = lax.all_gather(quad, 'zh', axis=0)  8.76 us
    ppermute x1, starting transfers between devices, per_device(): theirs = lax.ppermute(momentum.astype(BF16), 'zh', swap)  5.78 us
    ppermute x1, starting transfers between devices, per_device(): other = lax.ppermute(pack, 'c', swap)  5.35 us
    all_to_all x1, starting transfers between devices, per_device(): parts = lax.all_to_all(pair, 'x', 0, 0, tiled=True)  3.62 us
    all_to_all x1, waiting for transfers between devices, per_device(): parts = lax.all_to_all(pair, 'x', 0, 0, tiled=True)  3.52 us
  transfers between devices with their start and end apart: 5, of which 3 were waited for; matrix products, arithmetic and copies ran while one was open for 0% of the time, Pallas kernels for 2%

profile of v5, /device:TPU:1, one launch (start us, length us, event | category | flops | bytes accessed | tf_op | source)
XLA Modules:
  0.0 72.3 jit_solution(13077672848364131150)
XLA Ops:
  0.6 8.8 %collective-permute-start = (bf16[1,64,8192]{2,1,0:T(8,128)(2,1)}, bf16[1,64,8192]{2,1,0:T(8,128)(2,1)S(1)}, u32[]{:S(2)}, u32[]{:S(2)}) collective-permute-start(bf16[1,64,8192]{2,1,0:T(8,128)(2,1)} %local_ref.1), channel_id=1, source_target_pairs={{0,32},{32,0},{1,33},{33,1},{2,34},{34,2},{3,35},{35,3},{4,36},{36... | collective-permute-start | bytes 3145736 | tf_op jit(solution)/shard_map/ppermute | solution.py:194
  9.4 1.4 %fetch.1 = (bf16[4,64,1024]{2,1,0:T(8,128)(2,1)S(1)}, bf16[4,64,1024]{2,1,0:T(8,128)(2,1)S(1)}, f32[16,128]{1,0:T(8,128)S(1)}) custom-call(bf16[1,64,8192]{2,1,0:T(8,128)(2,1)} %local_ref.1, bf16[64,8192]{1,0:T(8,128)(2,1)} %refs_0_.1, f32[64,512]{1,0:T(8,128)} %refs_1_.1), custom_call_target="tpu_custom_call" | custom-call | bytes 4194304 | tf_op jit(solution)/shard_map/fetch/pallas_call | solution.py:72
  10.8 1.1 %collective-permute-done.got_ref = bf16[1,64,8192]{2,1,0:T(8,128)(2,1)S(1)} collective-permute-done((bf16[1,64,8192]{2,1,0:T(8,128)(2,1)}, bf16[1,64,8192]{2,1,0:T(8,128)(2,1)S(1)}, u32[]{:S(2)}, u32[]{:S(2)}) %collective-permute-start) | collective-permute-done | bytes 1048608 | tf_op jit(solution)/shard_map/ppermute | solution.py:194
  11.9 0.9 %pair.1 = bf16[4,528,128]{2,1,0:T(8,128)(2,1)} custom-call(bf16[4,64,1024]{2,1,0:T(8,128)(2,1)S(1)} %get-tuple-element.7.local_ref, bf16[4,64,1024]{2,1,0:T(8,128)(2,1)S(1)} %get-tuple-element.8.base_ref, f32[16,128]{1,0:T(8,128)S(1)} %get-tuple-element.9.rest_ref, bf16[1,64,8192]{2,1,0:T(8,128)(2,1)S(1)} %collective-permute-done.got_ref), custom_call_target="tpu_custom_call" | custom-call | tf_op jit(solution)/shard_map/pair/pallas_call | solution.py:196
  12.8 0.0 copy-start.1
  12.9 3.6 %all-to-all-start = ((bf16[4,528,128]{2,1,0:T(8,128)(2,1)}), bf16[4,528,128]{2,1,0:T(8,128)(2,1)S(1)}, u32[]{:S(2)}, u32[]{:S(2)}) async-start(bf16[4,528,128]{2,1,0:T(8,128)(2,1)} %pair.1), calls=%async_computation | async-start | bytes 1081344 | tf_op jit(solution)/shard_map/all_to_all | solution.py:202
  16.5 0.0 copy-done.1
  16.5 5.8 %collective-permute-start.1 = (bf16[64,512]{1,0:T(8,128)(2,1)S(1)}, bf16[64,512]{1,0:T(8,128)(2,1)S(1)}, u32[]{:S(2)}, u32[]{:S(2)}) collective-permute-start(bf16[64,512]{1,0:T(8,128)(2,1)S(1)} %convert_element_type.3), channel_id=1, source_target_pairs={{0,64},{64,0},{1,65},{65,1},{2,66},{66,2},{3,67},{67,3},{4,68},{68... | collective-permute-start | bytes 196616 | tf_op jit(solution)/shard_map/ppermute | solution.py:193
  22.3 3.5 %all-to-all-done.parts_ref = bf16[4,528,128]{2,1,0:T(8,128)(2,1)S(1)} async-done(((bf16[4,528,128]{2,1,0:T(8,128)(2,1)}), bf16[4,528,128]{2,1,0:T(8,128)(2,1)S(1)}, u32[]{:S(2)}, u32[]{:S(2)}) %all-to-all-start) | async-done | bytes 540704 | tf_op jit(solution)/shard_map/all_to_all | solution.py:202
  25.8 0.1 quad.1
  25.9 8.8 %all-gather = bf16[1152,128]{1,0:T(8,128)(2,1)S(1)} all-gather(bf16[576,128]{1,0:T(8,128)(2,1)S(1)} %quad.1), channel_id=2, replica_groups=mesh['x'=4,'zh'=2,'c'=2,'y'=8,'zl'=4] {'zh'}, dimensions={0}, use_global_device_ids=true | all-gather | bytes 442368 | tf_op jit(solution)/shard_map/all_gather | solution.py:207
  34.7 0.0 collective-permute-done.1.theirs_ref
  34.7 0.8 %total.1 = (bf16[992,128]{1,0:T(8,128)(2,1)S(1)}, f32[128,2]{1,0:T(8,128)}) custom-call(bf16[2,576,128]{2,1,0:T(8,128)(2,1)S(1)} %bitcast.7, f32[64,512]{1,0:T(8,128)S(1)} %copy-done.1, bf16[64,512]{1,0:T(8,128)(2,1)S(1)} %collective-permute-done.1.theirs_ref), custom_call_target="tpu_custom_call" | custom-call | tf_op jit(solution)/shard_map/total/pallas_call | solution.py:209
  35.5 13.8 %all-to-all-start.1 = ((f32[128,1,2]{2,1,0:T(1,128)}), f32[128,1,2]{2,1,0:T(1,128)S(1)}, u32[]{:S(2)}, u32[]{:S(2)}) async-start(f32[128,1,2]{2,1,0:T(1,128)} %bitcast.2), calls=%async_computation.1 | async-start | bytes 131072 | tf_op jit(solution)/shard_map/all_to_all | solution.py:215
  49.3 13.2 %all-gather.1 = bf16[3968,128]{1,0:T(8,128)(2,1)S(1)} all-gather(bf16[992,128]{1,0:T(8,128)(2,1)S(1)} %get-tuple-element.11), channel_id=3, replica_groups=mesh['x'=4,'zh'=2,'c'=2,'y'=8,'zl'=4] {'x'}, dimensions={0}, use_global_device_ids=true | all-gather | bytes 1269760 | tf_op jit(solution)/shard_map/all_gather | solution.py:216
  62.4 0.0 all-to-all-done.1
  62.4 0.0 copy-start
  62.4 0.2 pack.1.refs_2_
  62.7 5.4 %collective-permute-start.2 = (bf16[4144,128]{1,0:T(8,128)(2,1)S(1)}, bf16[4144,128]{1,0:T(8,128)(2,1)S(1)}, u32[]{:S(2)}, u32[]{:S(2)}) collective-permute-start(bf16[4144,128]{1,0:T(8,128)(2,1)S(1)} %pack.1.refs_2_), channel_id=1, source_target_pairs={{0,32},{32,0},{1,33},{33,1},{2,34},{34,2},{3,35},{35,3},{4,36},{36... | collective-permute-start | bytes 3182600 | tf_op jit(solution)/shard_map/ppermute | solution.py:221
  68.0 2.3 %collective-permute-done.2.refs_3_ = bf16[4144,128]{1,0:T(8,128)(2,1)S(1)} collective-permute-done((bf16[4144,128]{1,0:T(8,128)(2,1)S(1)}, bf16[4144,128]{1,0:T(8,128)(2,1)S(1)}, u32[]{:S(2)}, u32[]{:S(2)}) %collective-permute-start.2) | collective-permute-done | bytes 1060896 | tf_op jit(solution)/shard_map/ppermute | solution.py:221
  70.3 0.0 copy-done
  70.3 2.0 %final.1 = (bf16[64,8192]{1,0:T(8,128)(2,1)}, f32[64,512]{1,0:T(8,128)}) custom-call(bf16[64,8192]{1,0:T(8,128)(2,1)S(1)} %copy-done, f32[64,512]{1,0:T(8,128)S(1)} %copy-done.1, bf16[4144,128]{1,0:T(8,128)(2,1)S(1)} %pack.1.refs_2_, bf16[4144,128]{1,0:T(8,128)(2,1)S(1)} %collective-permute-done.2.refs_3_), custom_call_target="tpu_custom_call" | custom-call | tf_op jit(solution)/shard_map/final/pallas_call | solution.py:223
  (1 shorter events, 0.0 us)
Async XLA Ops:
  0.6 11.3 %collective-permute-start = (bf16[1,64,8192]{2,1,0:T(8,128)(2,1)}, bf16[1,64,8192]{2,1,0:T(8,128)(2,1)S(1)}, u32[]{:S(2)}, u32[]{:S(2)}) collective-permute-start(bf16[1,64,8192]{2,1,0:T(8,128)(2,1)} %local_ref.1), channel_id=1, source_target_pairs={{0,32},{32,0},{1,33},{33,1},{2,34},{34,2},{3,35},{35,3},{4,36},{36... | collective-permute-start | bytes 3145736 | tf_op jit(solution)/shard_map/ppermute | solution.py:194
  12.8 3.6 %copy-start.1 = (f32[64,512]{1,0:T(8,128)S(1)}, f32[64,512]{1,0:T(8,128)}, u32[]{:S(2)}) copy-start(f32[64,512]{1,0:T(8,128)} %refs_1_.1) | copy-start | bytes 393220
  12.9 13.0 %all-to-all-start = ((bf16[4,528,128]{2,1,0:T(8,128)(2,1)}), bf16[4,528,128]{2,1,0:T(8,128)(2,1)S(1)}, u32[]{:S(2)}, u32[]{:S(2)}) async-start(bf16[4,528,128]{2,1,0:T(8,128)(2,1)} %pair.1), calls=%async_computation | async-start | bytes 1081344 | tf_op jit(solution)/shard_map/all_to_all | solution.py:202
  16.5 18.2 %collective-permute-start.1 = (bf16[64,512]{1,0:T(8,128)(2,1)S(1)}, bf16[64,512]{1,0:T(8,128)(2,1)S(1)}, u32[]{:S(2)}, u32[]{:S(2)}) collective-permute-start(bf16[64,512]{1,0:T(8,128)(2,1)S(1)} %convert_element_type.3), channel_id=1, source_target_pairs={{0,64},{64,0},{1,65},{65,1},{2,66},{66,2},{3,67},{67,3},{4,68},{68... | collective-permute-start | bytes 196616 | tf_op jit(solution)/shard_map/ppermute | solution.py:193
  35.5 27.0 %all-to-all-start.1 = ((f32[128,1,2]{2,1,0:T(1,128)}), f32[128,1,2]{2,1,0:T(1,128)S(1)}, u32[]{:S(2)}, u32[]{:S(2)}) async-start(f32[128,1,2]{2,1,0:T(1,128)} %bitcast.2), calls=%async_computation.1 | async-start | bytes 131072 | tf_op jit(solution)/shard_map/all_to_all | solution.py:215
  62.4 7.9 %copy-start = (bf16[64,8192]{1,0:T(8,128)(2,1)S(1)}, bf16[64,8192]{1,0:T(8,128)(2,1)}, u32[]{:S(2)}) copy-start(bf16[64,8192]{1,0:T(8,128)(2,1)} %refs_0_.1) | copy-start | bytes 3145732
  62.7 7.6 %collective-permute-start.2 = (bf16[4144,128]{1,0:T(8,128)(2,1)S(1)}, bf16[4144,128]{1,0:T(8,128)(2,1)S(1)}, u32[]{:S(2)}, u32[]{:S(2)}) collective-permute-start(bf16[4144,128]{1,0:T(8,128)(2,1)S(1)} %pack.1.refs_2_), channel_id=1, source_target_pairs={{0,32},{32,0},{1,33},{33,1},{2,34},{34,2},{3,35},{35,3},{4,36},{36... | collective-permute-start | bytes 3182600 | tf_op jit(solution)/shard_map/ppermute | solution.py:221

commit v6 on v5

--- a/solution.py
+++ b/solution.py
@@ -16,13 +16,14 @@
 TILES = OWN // LANES
 SUMS = NZ * TILES * ROWS
 MOM = TILES * ROWS
-REST = 16
-MOST = MOM - REST
-QUAD = SUMS + NX * REST
-GATHER = SUMS + NZ * MOST
 TILE = 16
+HALF = TILE // 2
+MAIN = MOM - TILE
+QUAD = SUMS + NX * HALF
+LAST = SUMS + NZ * MAIN
+GATHER = LAST + TILE
 RESTS = NX * GATHER
-SCALARS = RESTS + NZ * NX * REST
+SCALARS = RESTS + NZ * NX * HALF
 PACK = SCALARS + 3 * TILE
 F32, BF16 = jnp.float32, jnp.bfloat16
 VMEM = pl.BlockSpec(memory_space=pltpu.VMEM)
@@ -50,7 +51,7 @@
     core = lax.axis_index("c")
     copies = [
         pltpu.make_async_copy(
-            mom_ref.at[ROWS - REST:, OWN - LANES:], rest_out, sems.at[2 * NX * NZ]
+            mom_ref.at[ROWS - TILE:, OWN - LANES:], rest_out, sems.at[2 * NX * NZ]
         )
     ]
     for x in range(NX):
@@ -73,7 +74,7 @@
         fetch_kernel,
         in_specs=[HBM] * 3,
         out_specs=[VMEM] * 3,
-        out_shape=[half, half, pltpu.VMEM((REST, LANES), F32)],
+        out_shape=[half, half, pltpu.VMEM((TILE, LANES), F32)],
         scratch_shapes=[pltpu.SemaphoreType.DMA((2 * NX * NZ + 1,))],
         cost_estimate=pl.CostEstimate(flops=0, bytes_accessed=2**22, transcendentals=0),
         compiler_params=SMALL,
@@ -105,9 +106,10 @@
         for k in range(1, NX):
             total = total + parts_ref[k, flat(t), :].astype(F32)
         out_ref[flat(t), :] = total.astype(BF16)
-    for k in range(NX):
-        at = SUMS + k * REST
-        out_ref[at:at + REST, :] = parts_ref[k, SUMS:, :]
+    for k in range(0, NX, 2):
+        last = [parts_ref[k + i, SUMS:, :].astype(F32)[HALF:] for i in range(2)]
+        at = SUMS + k * HALF
+        out_ref[at:at + TILE, :] = jnp.concatenate(last, axis=0).astype(BF16)
 
 
 def total_kernel(both_ref, mine_ref, theirs_ref, out_ref, squares_ref, buf, sem):
@@ -121,13 +123,18 @@
     copy = pltpu.make_async_copy(buf, squares_ref, sem)
     copy.start()
     half = lax.axis_index("zh")
+    last = []
     for t in range(TILES):
-        rows = ROWS - REST if t == TILES - 1 else ROWS
-        mine = mine_ref[:rows, t * LANES:(t + 1) * LANES].astype(BF16)
-        theirs = theirs_ref[:rows, t * LANES:(t + 1) * LANES]
-        for h in range(NZ):
-            at = SUMS + h * MOST + t * ROWS
-            out_ref[at:at + rows, :] = jnp.where(half == h, mine, theirs)
+        rows = ROWS - TILE if t == TILES - 1 else ROWS
+        cols = slice(t * LANES, (t + 1) * LANES)
+        mine, theirs = mine_ref[:, cols], theirs_ref[:, cols].astype(F32)
+        for h in range(NZ):
+            mom = jnp.where(half == h, mine, theirs)
+            at = SUMS + h * MAIN + t * ROWS
+            out_ref[at:at + rows, :] = mom[:rows].astype(BF16)
+            if rows < ROWS:
+                last.append(mom[rows:rows + HALF])
+    out_ref[LAST:, :] = jnp.concatenate(last, axis=0).astype(BF16)
     copy.wait()
 
 
@@ -135,8 +142,8 @@
     for x in range(NX):
         out_ref[x * GATHER:(x + 1) * GATHER, :] = own_ref[x]
     for h in range(NZ):
-        at = RESTS + h * NX * REST
-        out_ref[at:at + NX * REST, :] = both_ref[h, SUMS:, :]
+        at = RESTS + h * NX * HALF
+        out_ref[at:at + NX * HALF, :] = both_ref[h, SUMS:, :]
     left = jnp.broadcast_to(jnp.sum(shares_ref[:, 0:1]), (TILE, LANES))
     for k in range(3):
         part = left.astype(BF16)
@@ -156,7 +163,7 @@
 
     def weights(rows, cols, total, mom):
         scaled = (total.astype(F32).reshape(-1, 8, LANES) * sum_weight[None]).reshape(-1, LANES)
-        update = scaled + (0.7 * 0.81) * mom.astype(F32)
+        update = scaled + (0.7 * 0.81) * mom
         buf[rows, cols] = (base_ref[rows, cols].astype(F32) - update).astype(BF16)
 
     copies = []
@@ -167,12 +174,17 @@
                 for t in range(TILES):
                     cols = block_cols(x, h, owner, t)
                     at = x * GATHER + (h * TILES + t) * ROWS
-                    mom_at = x * GATHER + SUMS + h * MOST + t * ROWS
-                    rows = ROWS - REST if t == TILES - 1 else ROWS
-                    weights(slice(0, rows), cols, pack[at:at + rows, :], pack[mom_at:mom_at + rows, :])
+                    mom_at = x * GATHER + SUMS + h * MAIN + t * ROWS
+                    rows = ROWS - TILE if t == TILES - 1 else ROWS
+                    mom = pack[mom_at:mom_at + rows, :].astype(F32)
+                    weights(slice(0, rows), cols, pack[at:at + rows, :], mom)
                     if rows < ROWS:
-                        rest_at = RESTS + (h * NX + x) * REST
-                        weights(slice(rows, ROWS), cols, pack[at + rows:at + ROWS, :], pack[rest_at:rest_at + REST, :])
+                        last_at = x * GATHER + LAST
+                        rest_at = RESTS + (h * NX + x) // 2 * TILE
+                        last = pack[last_at:last_at + TILE, :].astype(F32)[h * HALF:(h + 1) * HALF]
+                        rest = pack[rest_at:rest_at + TILE, :].astype(F32)[x % 2 * HALF:(x % 2 + 1) * HALF]
+                        mom = jnp.concatenate([last, rest], axis=0)
+                        weights(slice(rows, ROWS), cols, pack[at + rows:at + ROWS, :], mom)
             at = (x * NZ + h) * NC * OWN
             cols = slice(at, at + NC * OWN)
             copies.append(pltpu.make_async_copy(buf.at[:, cols], new_ref.at[:, cols], sems.at[x * NZ + h]))
@@ -195,8 +207,8 @@
     mine, base, rest = fetch(local_weights, global_weights, momentum)
     pair = pl.pallas_call(
         pair_kernel, in_specs=[VMEM] * 4, out_specs=HBM,
-        out_shape=jax.ShapeDtypeStruct((NX, SUMS + REST, LANES), BF16),
-        scratch_shapes=[pltpu.VMEM((NX, SUMS + REST, LANES), BF16), pltpu.SemaphoreType.DMA((NX,))],
+        out_shape=jax.ShapeDtypeStruct((NX, SUMS + TILE, LANES), BF16),
+        scratch_shapes=[pltpu.VMEM((NX, SUMS + TILE, LANES), BF16), pltpu.SemaphoreType.DMA((NX,))],
         compiler_params=SMALL, name="pair",
     )(near(mine), near(base), near(rest), near(got))
     parts = lax.all_to_all(pair, "x", 0, 0, tiled=True)
@@ -208,8 +220,8 @@
     group = NX * NY * NL
     total, squares = pl.pallas_call(
         total_kernel, in_specs=[VMEM] * 3, out_specs=[VMEM, HBM],
-        out_shape=[pltpu.VMEM((GATHER, LANES), BF16), jax.ShapeDtypeStruct((group, 2), F32)],
-        scratch_shapes=[pltpu.VMEM((group, 2), F32), pltpu.SemaphoreType.DMA],
+        out_shape=[pltpu.VMEM((GATHER, LANES), BF16), jax.ShapeDtypeStruct((group, 128), F32)],
+        scratch_shapes=[pltpu.VMEM((group, 128), F32), pltpu.SemaphoreType.DMA],
         compiler_params=SMALL, name="total",
     )(near(both), near(momentum), near(theirs))
     shares = lax.all_to_all(squares, ("x", "y", "zl"), 0, 0, tiled=True)

time: 72.7 us -> 72.5 us (level)
  no operation moved by 1% of the time
where the time goes in v6:
time: 72.5 us; the launch traced here: 72.1 us
  starting transfers between devices  37.4 us (52%)
  blocking collectives  21.6 us (30%)
  waiting for transfers between devices  6.87 us (9%)
  Pallas kernels  5.4 us (7%)
  between operations  0.73 us (1%)
    all_to_all x1, starting transfers between devices, per_device(): shares = lax.all_to_all(squares, ('x', 'y', 'zl'), 0, 0, tiled=True)  13.6 us
    all_gather x1, blocking collectives, per_device(): own = lax.all_gather(total, 'x', axis=0)  13 us
    ppermute x1, starting transfers between devices, per_device(): got = lax.ppermute(local_weights, 'c', swap)  8.79 us
    all_gather x1, blocking collectives, per_device(): both = lax.all_gather(quad, 'zh', axis=0)  8.59 us
    ppermute x1, starting transfers between devices, per_device(): theirs = lax.ppermute(momentum.astype(BF16), 'zh', swap)  5.78 us
    ppermute x1, starting transfers between devices, per_device(): other = lax.ppermute(pack, 'c', swap)  5.7 us
    all_to_all x1, starting transfers between devices, per_device(): parts = lax.all_to_all(pair, 'x', 0, 0, tiled=True)  3.62 us
    all_to_all x1, waiting for transfers between devices, per_device(): parts = lax.all_to_all(pair, 'x', 0, 0, tiled=True)  3.52 us
  transfers between devices with their start and end apart: 5, of which 3 were waited for; matrix products, arithmetic and copies ran while one was open for 0% of the time, Pallas kernels for 2%

profile of v6, /device:TPU:1, one launch (start us, length us, event | category | flops | bytes accessed | tf_op | source)
XLA Modules:
  0.0 72.1 jit_solution(12792692044639203668)
XLA Ops:
  0.6 8.8 %collective-permute-start = (bf16[1,64,8192]{2,1,0:T(8,128)(2,1)}, bf16[1,64,8192]{2,1,0:T(8,128)(2,1)S(1)}, u32[]{:S(2)}, u32[]{:S(2)}) collective-permute-start(bf16[1,64,8192]{2,1,0:T(8,128)(2,1)} %local_ref.1), channel_id=1, source_target_pairs={{0,32},{32,0},{1,33},{33,1},{2,34},{34,2},{3,35},{35,3},{4,36},{36... | collective-permute-start | bytes 3145736 | tf_op jit(solution)/shard_map/ppermute | solution.py:206
  9.4 1.4 %fetch.1 = (bf16[4,64,1024]{2,1,0:T(8,128)(2,1)S(1)}, bf16[4,64,1024]{2,1,0:T(8,128)(2,1)S(1)}, f32[16,128]{1,0:T(8,128)S(1)}) custom-call(bf16[1,64,8192]{2,1,0:T(8,128)(2,1)} %local_ref.1, bf16[64,8192]{1,0:T(8,128)(2,1)} %refs_0_.1, f32[64,512]{1,0:T(8,128)} %refs_1_.1), custom_call_target="tpu_custom_call" | custom-call | bytes 4194304 | tf_op jit(solution)/shard_map/fetch/pallas_call | solution.py:73
  10.8 1.1 %collective-permute-done.got_ref = bf16[1,64,8192]{2,1,0:T(8,128)(2,1)S(1)} collective-permute-done((bf16[1,64,8192]{2,1,0:T(8,128)(2,1)}, bf16[1,64,8192]{2,1,0:T(8,128)(2,1)S(1)}, u32[]{:S(2)}, u32[]{:S(2)}) %collective-permute-start) | collective-permute-done | bytes 1048608 | tf_op jit(solution)/shard_map/ppermute | solution.py:206
  11.9 0.9 %pair.1 = bf16[4,528,128]{2,1,0:T(8,128)(2,1)} custom-call(bf16[4,64,1024]{2,1,0:T(8,128)(2,1)S(1)} %get-tuple-element.7.local_ref, bf16[4,64,1024]{2,1,0:T(8,128)(2,1)S(1)} %get-tuple-element.8.base_ref, f32[16,128]{1,0:T(8,128)S(1)} %get-tuple-element.9.rest_ref, bf16[1,64,8192]{2,1,0:T(8,128)(2,1)S(1)} %collective-permute-done.got_ref), custom_call_target="tpu_custom_call" | custom-call | tf_op jit(solution)/shard_map/pair/pallas_call | solution.py:208
  12.8 0.0 copy-start.1
  12.9 3.6 %all-to-all-start = ((bf16[4,528,128]{2,1,0:T(8,128)(2,1)}), bf16[4,528,128]{2,1,0:T(8,128)(2,1)S(1)}, u32[]{:S(2)}, u32[]{:S(2)}) async-start(bf16[4,528,128]{2,1,0:T(8,128)(2,1)} %pair.1), calls=%async_computation | async-start | bytes 1081344 | tf_op jit(solution)/shard_map/all_to_all | solution.py:214
  16.5 0.0 copy-done.1
  16.5 5.8 %collective-permute-start.1 = (bf16[64,512]{1,0:T(8,128)(2,1)S(1)}, bf16[64,512]{1,0:T(8,128)(2,1)S(1)}, u32[]{:S(2)}, u32[]{:S(2)}) collective-permute-start(bf16[64,512]{1,0:T(8,128)(2,1)S(1)} %convert_element_type.3), channel_id=1, source_target_pairs={{0,64},{64,0},{1,65},{65,1},{2,66},{66,2},{3,67},{67,3},{4,68},{68... | collective-permute-start | bytes 196616 | tf_op jit(solution)/shard_map/ppermute | solution.py:205
  22.3 3.5 %all-to-all-done.parts_ref = bf16[4,528,128]{2,1,0:T(8,128)(2,1)S(1)} async-done(((bf16[4,528,128]{2,1,0:T(8,128)(2,1)}), bf16[4,528,128]{2,1,0:T(8,128)(2,1)S(1)}, u32[]{:S(2)}, u32[]{:S(2)}) %all-to-all-start) | async-done | bytes 540704 | tf_op jit(solution)/shard_map/all_to_all | solution.py:214
  25.8 0.1 quad.1
  25.9 8.6 %all-gather = bf16[1088,128]{1,0:T(8,128)(2,1)S(1)} all-gather(bf16[544,128]{1,0:T(8,128)(2,1)S(1)} %quad.1), channel_id=2, replica_groups=mesh['x'=4,'zh'=2,'c'=2,'y'=8,'zl'=4] {'zh'}, dimensions={0}, use_global_device_ids=true | all-gather | bytes 417792 | tf_op jit(solution)/shard_map/all_gather | solution.py:219
  34.5 0.0 collective-permute-done.1.theirs_ref
  34.5 0.8 %total.1 = (bf16[1008,128]{1,0:T(8,128)(2,1)S(1)}, f32[128,128]{1,0:T(8,128)}) custom-call(bf16[2,544,128]{2,1,0:T(8,128)(2,1)S(1)} %bitcast.7, f32[64,512]{1,0:T(8,128)S(1)} %copy-done.1, bf16[64,512]{1,0:T(8,128)(2,1)S(1)} %collective-permute-done.1.theirs_ref), custom_call_target="tpu_custom_call" | custom-call | tf_op jit(solution)/shard_map/total/pallas_call | solution.py:221
  35.3 13.6 %all-to-all-start.1 = ((f32[128,1,128]{2,1,0:T(1,128)}), f32[128,1,128]{2,1,0:T(1,128)S(1)}, u32[]{:S(2)}, u32[]{:S(2)}) async-start(f32[128,1,128]{2,1,0:T(1,128)} %bitcast.2), calls=%async_computation.1 | async-start | bytes 131072 | tf_op jit(solution)/shard_map/all_to_all | solution.py:227
  48.9 13.0 %all-gather.1 = bf16[4032,128]{1,0:T(8,128)(2,1)S(1)} all-gather(bf16[1008,128]{1,0:T(8,128)(2,1)S(1)} %get-tuple-element.11), channel_id=3, replica_groups=mesh['x'=4,'zh'=2,'c'=2,'y'=8,'zl'=4] {'x'}, dimensions={0}, use_global_device_ids=true | all-gather | bytes 1290240 | tf_op jit(solution)/shard_map/all_gather | solution.py:228
  61.9 0.0 all-to-all-done.1
  61.9 0.0 copy-start
  61.9 0.2 pack.1.refs_2_
  62.1 5.7 %collective-permute-start.2 = (bf16[4144,128]{1,0:T(8,128)(2,1)S(1)}, bf16[4144,128]{1,0:T(8,128)(2,1)S(1)}, u32[]{:S(2)}, u32[]{:S(2)}) collective-permute-start(bf16[4144,128]{1,0:T(8,128)(2,1)S(1)} %pack.1.refs_2_), channel_id=1, source_target_pairs={{0,32},{32,0},{1,33},{33,1},{2,34},{34,2},{3,35},{35,3},{4,36},{36... | collective-permute-start | bytes 3182600 | tf_op jit(solution)/shard_map/ppermute | solution.py:233
  67.8 2.3 %collective-permute-done.2.refs_3_ = bf16[4144,128]{1,0:T(8,128)(2,1)S(1)} collective-permute-done((bf16[4144,128]{1,0:T(8,128)(2,1)S(1)}, bf16[4144,128]{1,0:T(8,128)(2,1)S(1)}, u32[]{:S(2)}, u32[]{:S(2)}) %collective-permute-start.2) | collective-permute-done | bytes 1060896 | tf_op jit(solution)/shard_map/ppermute | solution.py:233
  70.1 0.0 copy-done
  70.1 2.0 %final.1 = (bf16[64,8192]{1,0:T(8,128)(2,1)}, f32[64,512]{1,0:T(8,128)}) custom-call(bf16[64,8192]{1,0:T(8,128)(2,1)S(1)} %copy-done, f32[64,512]{1,0:T(8,128)S(1)} %copy-done.1, bf16[4144,128]{1,0:T(8,128)(2,1)S(1)} %pack.1.refs_2_, bf16[4144,128]{1,0:T(8,128)(2,1)S(1)} %collective-permute-done.2.refs_3_), custom_call_target="tpu_custom_call" | custom-call | tf_op jit(solution)/shard_map/final/pallas_call | solution.py:235
  (1 shorter events, 0.0 us)
Async XLA Ops:
  0.6 11.3 %collective-permute-start = (bf16[1,64,8192]{2,1,0:T(8,128)(2,1)}, bf16[1,64,8192]{2,1,0:T(8,128)(2,1)S(1)}, u32[]{:S(2)}, u32[]{:S(2)}) collective-permute-start(bf16[1,64,8192]{2,1,0:T(8,128)(2,1)} %local_ref.1), channel_id=1, source_target_pairs={{0,32},{32,0},{1,33},{33,1},{2,34},{34,2},{3,35},{35,3},{4,36},{36... | collective-permute-start | bytes 3145736 | tf_op jit(solution)/shard_map/ppermute | solution.py:206
  12.8 3.6 %copy-start.1 = (f32[64,512]{1,0:T(8,128)S(1)}, f32[64,512]{1,0:T(8,128)}, u32[]{:S(2)}) copy-start(f32[64,512]{1,0:T(8,128)} %refs_1_.1) | copy-start | bytes 393220
  12.9 13.0 %all-to-all-start = ((bf16[4,528,128]{2,1,0:T(8,128)(2,1)}), bf16[4,528,128]{2,1,0:T(8,128)(2,1)S(1)}, u32[]{:S(2)}, u32[]{:S(2)}) async-start(bf16[4,528,128]{2,1,0:T(8,128)(2,1)} %pair.1), calls=%async_computation | async-start | bytes 1081344 | tf_op jit(solution)/shard_map/all_to_all | solution.py:214
  16.5 18.0 %collective-permute-start.1 = (bf16[64,512]{1,0:T(8,128)(2,1)S(1)}, bf16[64,512]{1,0:T(8,128)(2,1)S(1)}, u32[]{:S(2)}, u32[]{:S(2)}) collective-permute-start(bf16[64,512]{1,0:T(8,128)(2,1)S(1)} %convert_element_type.3), channel_id=1, source_target_pairs={{0,64},{64,0},{1,65},{65,1},{2,66},{66,2},{3,67},{67,3},{4,68},{68... | collective-permute-start | bytes 196616 | tf_op jit(solution)/shard_map/ppermute | solution.py:205
  35.3 26.6 %all-to-all-start.1 = ((f32[128,1,128]{2,1,0:T(1,128)}), f32[128,1,128]{2,1,0:T(1,128)S(1)}, u32[]{:S(2)}, u32[]{:S(2)}) async-start(f32[128,1,128]{2,1,0:T(1,128)} %bitcast.2), calls=%async_computation.1 | async-start | bytes 131072 | tf_op jit(solution)/shard_map/all_to_all | solution.py:227
  61.9 8.2 %copy-start = (bf16[64,8192]{1,0:T(8,128)(2,1)S(1)}, bf16[64,8192]{1,0:T(8,128)(2,1)}, u32[]{:S(2)}) copy-start(bf16[64,8192]{1,0:T(8,128)(2,1)} %refs_0_.1) | copy-start | bytes 3145732
  62.1 8.0 %collective-permute-start.2 = (bf16[4144,128]{1,0:T(8,128)(2,1)S(1)}, bf16[4144,128]{1,0:T(8,128)(2,1)S(1)}, u32[]{:S(2)}, u32[]{:S(2)}) collective-permute-start(bf16[4144,128]{1,0:T(8,128)(2,1)S(1)} %pack.1.refs_2_), channel_id=1, source_target_pairs={{0,32},{32,0},{1,33},{33,1},{2,34},{34,2},{3,35},{35,3},{4,36},{36... | collective-permute-start | bytes 3182600 | tf_op jit(solution)/shard_map/ppermute | solution.py:233

commit v7 on v6

--- a/solution.py
+++ b/solution.py
@@ -151,7 +151,7 @@
         left = left - part.astype(F32)
 
 
-def final_kernel(entries, base_ref, mom_ref, mine_ref, theirs_ref, new_ref, newmom_ref, buf, sems):
+def final_kernel(entries, base_ref, mom_ref, mine_ref, theirs_ref, new_ref, newmom_ref, buf, mom_buf, sems, mom_sem):
     core = lax.axis_index("c")
     squares = jnp.zeros((8, LANES), F32)
     for pack in (mine_ref, theirs_ref):
@@ -166,7 +166,14 @@
         update = scaled + (0.7 * 0.81) * mom
         buf[rows, cols] = (base_ref[rows, cols].astype(F32) - update).astype(BF16)
 
-    copies = []
+    for t in range(TILES):
+        at = lax.axis_index("x") * GATHER + (lax.axis_index("zh") * TILES + t) * ROWS
+        total = mine_ref[pl.ds(pl.multiple_of(at, TILE), ROWS), :].astype(F32)
+        cols = slice(t * LANES, (t + 1) * LANES)
+        scaled = (total.reshape(-1, 8, LANES) * factor[None]).reshape(-1, LANES)
+        mom_buf[:, cols] = 0.9 * mom_ref[:, cols] + scaled
+    copies = [pltpu.make_async_copy(mom_buf, newmom_ref, mom_sem)]
+    copies[0].start()
     for x in range(NX):
         for h in range(NZ):
             for which, pack in enumerate((mine_ref, theirs_ref)):
@@ -189,12 +196,6 @@
             cols = slice(at, at + NC * OWN)
             copies.append(pltpu.make_async_copy(buf.at[:, cols], new_ref.at[:, cols], sems.at[x * NZ + h]))
             copies[-1].start()
-    for t in range(TILES):
-        at = lax.axis_index("x") * GATHER + (lax.axis_index("zh") * TILES + t) * ROWS
-        total = mine_ref[pl.ds(pl.multiple_of(at, TILE), ROWS), :].astype(F32)
-        cols = slice(t * LANES, (t + 1) * LANES)
-        scaled = (total.reshape(-1, 8, LANES) * factor[None]).reshape(-1, LANES)
-        newmom_ref[:, cols] = 0.9 * mom_ref[:, cols] + scaled
     for copy in copies:
         copy.wait()
 
@@ -234,9 +235,12 @@
     entries = rows * width * NY * NL
     return pl.pallas_call(
         lambda *refs: final_kernel(entries, *refs),
-        in_specs=[VMEM] * 4, out_specs=[HBM, VMEM],
+        in_specs=[VMEM] * 4, out_specs=[HBM, HBM],
         out_shape=[jax.ShapeDtypeStruct((rows, width), BF16), jax.ShapeDtypeStruct(momentum.shape, F32)],
-        scratch_shapes=[pltpu.VMEM((rows, width), BF16), pltpu.SemaphoreType.DMA((NX * NZ,))],
+        scratch_shapes=[
+            pltpu.VMEM((rows, width), BF16), pltpu.VMEM(momentum.shape, F32),
+            pltpu.SemaphoreType.DMA((NX * NZ,)), pltpu.SemaphoreType.DMA,
+        ],
         compiler_params=SMALL, name="final",
     )(near(global_weights), near(momentum), near(pack), near(other))
 

time: 72.5 us -> 71.8 us (level)
  no operation moved by 1% of the time
where the time goes in v7:
time: 71.8 us; the launch traced here: 71.5 us
  starting transfers between devices  37.4 us (52%)
  blocking collectives  21.6 us (30%)
  waiting for transfers between devices  6.87 us (10%)
  Pallas kernels  4.78 us (7%)
  between operations  0.73 us (1%)
    all_to_all x1, starting transfers between devices, per_device(): shares = lax.all_to_all(squares, ('x', 'y', 'zl'), 0, 0, tiled=True)  13.6 us
    all_gather x1, blocking collectives, per_device(): own = lax.all_gather(total, 'x', axis=0)  13 us
    ppermute x1, starting transfers between devices, per_device(): got = lax.ppermute(local_weights, 'c', swap)  8.79 us
    all_gather x1, blocking collectives, per_device(): both = lax.all_gather(quad, 'zh', axis=0)  8.59 us
    ppermute x1, starting transfers between devices, per_device(): theirs = lax.ppermute(momentum.astype(BF16), 'zh', swap)  5.78 us
    ppermute x1, starting transfers between devices, per_device(): other = lax.ppermute(pack, 'c', swap)  5.7 us
    all_to_all x1, starting transfers between devices, per_device(): parts = lax.all_to_all(pair, 'x', 0, 0, tiled=True)  3.62 us
    all_to_all x1, waiting for transfers between devices, per_device(): parts = lax.all_to_all(pair, 'x', 0, 0, tiled=True)  3.52 us
  transfers between devices with their start and end apart: 5, of which 3 were waited for; matrix products, arithmetic and copies ran while one was open for 0% of the time, Pallas kernels for 2%

profile of v7, /device:TPU:1, one launch (start us, length us, event | category | flops | bytes accessed | tf_op | source)
XLA Modules:
  0.0 71.5 jit_solution(7341420182956244398)
XLA Ops:
  0.6 8.8 %collective-permute-start = (bf16[1,64,8192]{2,1,0:T(8,128)(2,1)}, bf16[1,64,8192]{2,1,0:T(8,128)(2,1)S(1)}, u32[]{:S(2)}, u32[]{:S(2)}) collective-permute-start(bf16[1,64,8192]{2,1,0:T(8,128)(2,1)} %local_ref.1), channel_id=1, source_target_pairs={{0,32},{32,0},{1,33},{33,1},{2,34},{34,2},{3,35},{35,3},{4,36},{36... | collective-permute-start | bytes 3145736 | tf_op jit(solution)/shard_map/ppermute | solution.py:207
  9.4 1.4 %fetch.1 = (bf16[4,64,1024]{2,1,0:T(8,128)(2,1)S(1)}, bf16[4,64,1024]{2,1,0:T(8,128)(2,1)S(1)}, f32[16,128]{1,0:T(8,128)S(1)}) custom-call(bf16[1,64,8192]{2,1,0:T(8,128)(2,1)} %local_ref.1, bf16[64,8192]{1,0:T(8,128)(2,1)} %refs_0_.1, f32[64,512]{1,0:T(8,128)} %refs_1_.1), custom_call_target="tpu_custom_call" | custom-call | bytes 4194304 | tf_op jit(solution)/shard_map/fetch/pallas_call | solution.py:73
  10.8 1.1 %collective-permute-done.got_ref = bf16[1,64,8192]{2,1,0:T(8,128)(2,1)S(1)} collective-permute-done((bf16[1,64,8192]{2,1,0:T(8,128)(2,1)}, bf16[1,64,8192]{2,1,0:T(8,128)(2,1)S(1)}, u32[]{:S(2)}, u32[]{:S(2)}) %collective-permute-start) | collective-permute-done | bytes 1048608 | tf_op jit(solution)/shard_map/ppermute | solution.py:207
  11.9 0.9 %pair.1 = bf16[4,528,128]{2,1,0:T(8,128)(2,1)} custom-call(bf16[4,64,1024]{2,1,0:T(8,128)(2,1)S(1)} %get-tuple-element.7.local_ref, bf16[4,64,1024]{2,1,0:T(8,128)(2,1)S(1)} %get-tuple-element.8.base_ref, f32[16,128]{1,0:T(8,128)S(1)} %get-tuple-element.9.rest_ref, bf16[1,64,8192]{2,1,0:T(8,128)(2,1)S(1)} %collective-permute-done.got_ref), custom_call_target="tpu_custom_call" | custom-call | tf_op jit(solution)/shard_map/pair/pallas_call | solution.py:209
  12.8 0.0 copy-start.1
  12.9 3.6 %all-to-all-start = ((bf16[4,528,128]{2,1,0:T(8,128)(2,1)}), bf16[4,528,128]{2,1,0:T(8,128)(2,1)S(1)}, u32[]{:S(2)}, u32[]{:S(2)}) async-start(bf16[4,528,128]{2,1,0:T(8,128)(2,1)} %pair.1), calls=%async_computation | async-start | bytes 1081344 | tf_op jit(solution)/shard_map/all_to_all | solution.py:215
  16.5 0.0 copy-done.1
  16.5 5.8 %collective-permute-start.1 = (bf16[64,512]{1,0:T(8,128)(2,1)S(1)}, bf16[64,512]{1,0:T(8,128)(2,1)S(1)}, u32[]{:S(2)}, u32[]{:S(2)}) collective-permute-start(bf16[64,512]{1,0:T(8,128)(2,1)S(1)} %convert_element_type.3), channel_id=1, source_target_pairs={{0,64},{64,0},{1,65},{65,1},{2,66},{66,2},{3,67},{67,3},{4,68},{68... | collective-permute-start | bytes 196616 | tf_op jit(solution)/shard_map/ppermute | solution.py:206
  22.3 3.5 %all-to-all-done.parts_ref = bf16[4,528,128]{2,1,0:T(8,128)(2,1)S(1)} async-done(((bf16[4,528,128]{2,1,0:T(8,128)(2,1)}), bf16[4,528,128]{2,1,0:T(8,128)(2,1)S(1)}, u32[]{:S(2)}, u32[]{:S(2)}) %all-to-all-start) | async-done | bytes 540704 | tf_op jit(solution)/shard_map/all_to_all | solution.py:215
  25.8 0.1 quad.1
  25.9 8.6 %all-gather = bf16[1088,128]{1,0:T(8,128)(2,1)S(1)} all-gather(bf16[544,128]{1,0:T(8,128)(2,1)S(1)} %quad.1), channel_id=2, replica_groups=mesh['x'=4,'zh'=2,'c'=2,'y'=8,'zl'=4] {'zh'}, dimensions={0}, use_global_device_ids=true | all-gather | bytes 417792 | tf_op jit(solution)/shard_map/all_gather | solution.py:220
  34.5 0.0 collective-permute-done.1.theirs_ref
  34.5 0.8 %total.1 = (bf16[1008,128]{1,0:T(8,128)(2,1)S(1)}, f32[128,128]{1,0:T(8,128)}) custom-call(bf16[2,544,128]{2,1,0:T(8,128)(2,1)S(1)} %bitcast.7, f32[64,512]{1,0:T(8,128)S(1)} %copy-done.1, bf16[64,512]{1,0:T(8,128)(2,1)S(1)} %collective-permute-done.1.theirs_ref), custom_call_target="tpu_custom_call" | custom-call | tf_op jit(solution)/shard_map/total/pallas_call | solution.py:222
  35.3 13.6 %all-to-all-start.1 = ((f32[128,1,128]{2,1,0:T(1,128)}), f32[128,1,128]{2,1,0:T(1,128)S(1)}, u32[]{:S(2)}, u32[]{:S(2)}) async-start(f32[128,1,128]{2,1,0:T(1,128)} %bitcast.2), calls=%async_computation.1 | async-start | bytes 131072 | tf_op jit(solution)/shard_map/all_to_all | solution.py:228
  48.9 13.0 %all-gather.1 = bf16[4032,128]{1,0:T(8,128)(2,1)S(1)} all-gather(bf16[1008,128]{1,0:T(8,128)(2,1)S(1)} %get-tuple-element.11), channel_id=3, replica_groups=mesh['x'=4,'zh'=2,'c'=2,'y'=8,'zl'=4] {'x'}, dimensions={0}, use_global_device_ids=true | all-gather | bytes 1290240 | tf_op jit(solution)/shard_map/all_gather | solution.py:229
  61.9 0.0 all-to-all-done.1
  61.9 0.0 copy-start
  61.9 0.2 pack.1.refs_2_
  62.1 5.7 %collective-permute-start.2 = (bf16[4144,128]{1,0:T(8,128)(2,1)S(1)}, bf16[4144,128]{1,0:T(8,128)(2,1)S(1)}, u32[]{:S(2)}, u32[]{:S(2)}) collective-permute-start(bf16[4144,128]{1,0:T(8,128)(2,1)S(1)} %pack.1.refs_2_), channel_id=1, source_target_pairs={{0,32},{32,0},{1,33},{33,1},{2,34},{34,2},{3,35},{35,3},{4,36},{36... | collective-permute-start | bytes 3182600 | tf_op jit(solution)/shard_map/ppermute | solution.py:234
  67.8 2.3 %collective-permute-done.2.refs_3_ = bf16[4144,128]{1,0:T(8,128)(2,1)S(1)} collective-permute-done((bf16[4144,128]{1,0:T(8,128)(2,1)S(1)}, bf16[4144,128]{1,0:T(8,128)(2,1)S(1)}, u32[]{:S(2)}, u32[]{:S(2)}) %collective-permute-start.2) | collective-permute-done | bytes 1060896 | tf_op jit(solution)/shard_map/ppermute | solution.py:234
  70.1 0.0 copy-done
  70.1 1.4 %final.1 = (bf16[64,8192]{1,0:T(8,128)(2,1)}, f32[64,512]{1,0:T(8,128)}) custom-call(bf16[64,8192]{1,0:T(8,128)(2,1)S(1)} %copy-done, f32[64,512]{1,0:T(8,128)S(1)} %copy-done.1, bf16[4144,128]{1,0:T(8,128)(2,1)S(1)} %pack.1.refs_2_, bf16[4144,128]{1,0:T(8,128)(2,1)S(1)} %collective-permute-done.2.refs_3_), custom_call_target="tpu_custom_call" | custom-call | tf_op jit(solution)/shard_map/final/pallas_call | solution.py:236
  (1 shorter events, 0.0 us)
Async XLA Ops:
  0.6 11.3 %collective-permute-start = (bf16[1,64,8192]{2,1,0:T(8,128)(2,1)}, bf16[1,64,8192]{2,1,0:T(8,128)(2,1)S(1)}, u32[]{:S(2)}, u32[]{:S(2)}) collective-permute-start(bf16[1,64,8192]{2,1,0:T(8,128)(2,1)} %local_ref.1), channel_id=1, source_target_pairs={{0,32},{32,0},{1,33},{33,1},{2,34},{34,2},{3,35},{35,3},{4,36},{36... | collective-permute-start | bytes 3145736 | tf_op jit(solution)/shard_map/ppermute | solution.py:207
  12.8 3.6 %copy-start.1 = (f32[64,512]{1,0:T(8,128)S(1)}, f32[64,512]{1,0:T(8,128)}, u32[]{:S(2)}) copy-start(f32[64,512]{1,0:T(8,128)} %refs_1_.1) | copy-start | bytes 393220
  12.9 13.0 %all-to-all-start = ((bf16[4,528,128]{2,1,0:T(8,128)(2,1)}), bf16[4,528,128]{2,1,0:T(8,128)(2,1)S(1)}, u32[]{:S(2)}, u32[]{:S(2)}) async-start(bf16[4,528,128]{2,1,0:T(8,128)(2,1)} %pair.1), calls=%async_computation | async-start | bytes 1081344 | tf_op jit(solution)/shard_map/all_to_all | solution.py:215
  16.5 18.0 %collective-permute-start.1 = (bf16[64,512]{1,0:T(8,128)(2,1)S(1)}, bf16[64,512]{1,0:T(8,128)(2,1)S(1)}, u32[]{:S(2)}, u32[]{:S(2)}) collective-permute-start(bf16[64,512]{1,0:T(8,128)(2,1)S(1)} %convert_element_type.3), channel_id=1, source_target_pairs={{0,64},{64,0},{1,65},{65,1},{2,66},{66,2},{3,67},{67,3},{4,68},{68... | collective-permute-start | bytes 196616 | tf_op jit(solution)/shard_map/ppermute | solution.py:206
  35.3 26.6 %all-to-all-start.1 = ((f32[128,1,128]{2,1,0:T(1,128)}), f32[128,1,128]{2,1,0:T(1,128)S(1)}, u32[]{:S(2)}, u32[]{:S(2)}) async-start(f32[128,1,128]{2,1,0:T(1,128)} %bitcast.2), calls=%async_computation.1 | async-start | bytes 131072 | tf_op jit(solution)/shard_map/all_to_all | solution.py:228
  61.9 8.2 %copy-start = (bf16[64,8192]{1,0:T(8,128)(2,1)S(1)}, bf16[64,8192]{1,0:T(8,128)(2,1)}, u32[]{:S(2)}) copy-start(bf16[64,8192]{1,0:T(8,128)(2,1)} %refs_0_.1) | copy-start | bytes 3145732
  62.1 8.0 %collective-permute-start.2 = (bf16[4144,128]{1,0:T(8,128)(2,1)S(1)}, bf16[4144,128]{1,0:T(8,128)(2,1)S(1)}, u32[]{:S(2)}, u32[]{:S(2)}) collective-permute-start(bf16[4144,128]{1,0:T(8,128)(2,1)S(1)} %pack.1.refs_2_), channel_id=1, source_target_pairs={{0,32},{32,0},{1,33},{33,1},{2,34},{34,2},{3,35},{35,3},{4,36},{36... | collective-permute-start | bytes 3182600 | tf_op jit(solution)/shard_map/ppermute | solution.py:234

commit v8 on v7

--- a/solution.py
+++ b/solution.py
@@ -192,10 +192,10 @@
                         rest = pack[rest_at:rest_at + TILE, :].astype(F32)[x % 2 * HALF:(x % 2 + 1) * HALF]
                         mom = jnp.concatenate([last, rest], axis=0)
                         weights(slice(rows, ROWS), cols, pack[at + rows:at + ROWS, :], mom)
-            at = (x * NZ + h) * NC * OWN
-            cols = slice(at, at + NC * OWN)
-            copies.append(pltpu.make_async_copy(buf.at[:, cols], new_ref.at[:, cols], sems.at[x * NZ + h]))
-            copies[-1].start()
+                block = (x * NZ + h) * NC
+                cols = pl.ds(pl.multiple_of((block + owner) * OWN, OWN), OWN)
+                copies.append(pltpu.make_async_copy(buf.at[:, cols], new_ref.at[:, cols], sems.at[block + which]))
+                copies[-1].start()
     for copy in copies:
         copy.wait()
 
@@ -239,7 +239,7 @@
         out_shape=[jax.ShapeDtypeStruct((rows, width), BF16), jax.ShapeDtypeStruct(momentum.shape, F32)],
         scratch_shapes=[
             pltpu.VMEM((rows, width), BF16), pltpu.VMEM(momentum.shape, F32),
-            pltpu.SemaphoreType.DMA((NX * NZ,)), pltpu.SemaphoreType.DMA,
+            pltpu.SemaphoreType.DMA((NX * NZ * NC,)), pltpu.SemaphoreType.DMA,
         ],
         compiler_params=SMALL, name="final",
     )(near(global_weights), near(momentum), near(pack), near(other))

time: 71.8 us -> 71.9 us (level)
  no operation moved by 1% of the time
where the time goes in v8:
time: 71.9 us; the launch traced here: 71.5 us
  starting transfers between devices  37.4 us (52%)
  blocking collectives  21.6 us (30%)
  waiting for transfers between devices  6.87 us (10%)
  Pallas kernels  4.82 us (7%)
  between operations  0.73 us (1%)
    all_to_all x1, starting transfers between devices, per_device(): shares = lax.all_to_all(squares, ('x', 'y', 'zl'), 0, 0, tiled=True)  13.6 us
    all_gather x1, blocking collectives, per_device(): own = lax.all_gather(total, 'x', axis=0)  13 us
    ppermute x1, starting transfers between devices, per_device(): got = lax.ppermute(local_weights, 'c', swap)  8.79 us
    all_gather x1, blocking collectives, per_device(): both = lax.all_gather(quad, 'zh', axis=0)  8.59 us
    ppermute x1, starting transfers between devices, per_device(): theirs = lax.ppermute(momentum.astype(BF16), 'zh', swap)  5.78 us
    ppermute x1, starting transfers between devices, per_device(): other = lax.ppermute(pack, 'c', swap)  5.7 us
    all_to_all x1, starting transfers between devices, per_device(): parts = lax.all_to_all(pair, 'x', 0, 0, tiled=True)  3.62 us
    all_to_all x1, waiting for transfers between devices, per_device(): parts = lax.all_to_all(pair, 'x', 0, 0, tiled=True)  3.52 us
  transfers between devices with their start and end apart: 5, of which 3 were waited for; matrix products, arithmetic and copies ran while one was open for 0% of the time, Pallas kernels for 2%

profile of v8, /device:TPU:1, one launch (start us, length us, event | category | flops | bytes accessed | tf_op | source)
XLA Modules:
  0.0 71.5 jit_solution(5214812592523932710)
XLA Ops:
  0.6 8.8 %collective-permute-start = (bf16[1,64,8192]{2,1,0:T(8,128)(2,1)}, bf16[1,64,8192]{2,1,0:T(8,128)(2,1)S(1)}, u32[]{:S(2)}, u32[]{:S(2)}) collective-permute-start(bf16[1,64,8192]{2,1,0:T(8,128)(2,1)} %local_ref.1), channel_id=1, source_target_pairs={{0,32},{32,0},{1,33},{33,1},{2,34},{34,2},{3,35},{35,3},{4,36},{36... | collective-permute-start | bytes 3145736 | tf_op jit(solution)/shard_map/ppermute | solution.py:207
  9.4 1.4 %fetch.1 = (bf16[4,64,1024]{2,1,0:T(8,128)(2,1)S(1)}, bf16[4,64,1024]{2,1,0:T(8,128)(2,1)S(1)}, f32[16,128]{1,0:T(8,128)S(1)}) custom-call(bf16[1,64,8192]{2,1,0:T(8,128)(2,1)} %local_ref.1, bf16[64,8192]{1,0:T(8,128)(2,1)} %refs_0_.1, f32[64,512]{1,0:T(8,128)} %refs_1_.1), custom_call_target="tpu_custom_call" | custom-call | bytes 4194304 | tf_op jit(solution)/shard_map/fetch/pallas_call | solution.py:73
  10.8 1.1 %collective-permute-done.got_ref = bf16[1,64,8192]{2,1,0:T(8,128)(2,1)S(1)} collective-permute-done((bf16[1,64,8192]{2,1,0:T(8,128)(2,1)}, bf16[1,64,8192]{2,1,0:T(8,128)(2,1)S(1)}, u32[]{:S(2)}, u32[]{:S(2)}) %collective-permute-start) | collective-permute-done | bytes 1048608 | tf_op jit(solution)/shard_map/ppermute | solution.py:207
  11.9 0.9 %pair.1 = bf16[4,528,128]{2,1,0:T(8,128)(2,1)} custom-call(bf16[4,64,1024]{2,1,0:T(8,128)(2,1)S(1)} %get-tuple-element.7.local_ref, bf16[4,64,1024]{2,1,0:T(8,128)(2,1)S(1)} %get-tuple-element.8.base_ref, f32[16,128]{1,0:T(8,128)S(1)} %get-tuple-element.9.rest_ref, bf16[1,64,8192]{2,1,0:T(8,128)(2,1)S(1)} %collective-permute-done.got_ref), custom_call_target="tpu_custom_call" | custom-call | tf_op jit(solution)/shard_map/pair/pallas_call | solution.py:209
  12.8 0.0 copy-start.1
  12.9 3.6 %all-to-all-start = ((bf16[4,528,128]{2,1,0:T(8,128)(2,1)}), bf16[4,528,128]{2,1,0:T(8,128)(2,1)S(1)}, u32[]{:S(2)}, u32[]{:S(2)}) async-start(bf16[4,528,128]{2,1,0:T(8,128)(2,1)} %pair.1), calls=%async_computation | async-start | bytes 1081344 | tf_op jit(solution)/shard_map/all_to_all | solution.py:215
  16.5 0.0 copy-done.1
  16.5 5.8 %collective-permute-start.1 = (bf16[64,512]{1,0:T(8,128)(2,1)S(1)}, bf16[64,512]{1,0:T(8,128)(2,1)S(1)}, u32[]{:S(2)}, u32[]{:S(2)}) collective-permute-start(bf16[64,512]{1,0:T(8,128)(2,1)S(1)} %convert_element_type.3), channel_id=1, source_target_pairs={{0,64},{64,0},{1,65},{65,1},{2,66},{66,2},{3,67},{67,3},{4,68},{68... | collective-permute-start | bytes 196616 | tf_op jit(solution)/shard_map/ppermute | solution.py:206
  22.3 3.5 %all-to-all-done.parts_ref = bf16[4,528,128]{2,1,0:T(8,128)(2,1)S(1)} async-done(((bf16[4,528,128]{2,1,0:T(8,128)(2,1)}), bf16[4,528,128]{2,1,0:T(8,128)(2,1)S(1)}, u32[]{:S(2)}, u32[]{:S(2)}) %all-to-all-start) | async-done | bytes 540704 | tf_op jit(solution)/shard_map/all_to_all | solution.py:215
  25.8 0.1 quad.1
  25.9 8.6 %all-gather = bf16[1088,128]{1,0:T(8,128)(2,1)S(1)} all-gather(bf16[544,128]{1,0:T(8,128)(2,1)S(1)} %quad.1), channel_id=2, replica_groups=mesh['x'=4,'zh'=2,'c'=2,'y'=8,'zl'=4] {'zh'}, dimensions={0}, use_global_device_ids=true | all-gather | bytes 417792 | tf_op jit(solution)/shard_map/all_gather | solution.py:220
  34.5 0.0 collective-permute-done.1.theirs_ref
  34.5 0.8 %total.1 = (bf16[1008,128]{1,0:T(8,128)(2,1)S(1)}, f32[128,128]{1,0:T(8,128)}) custom-call(bf16[2,544,128]{2,1,0:T(8,128)(2,1)S(1)} %bitcast.7, f32[64,512]{1,0:T(8,128)S(1)} %copy-done.1, bf16[64,512]{1,0:T(8,128)(2,1)S(1)} %collective-permute-done.1.theirs_ref), custom_call_target="tpu_custom_call" | custom-call | tf_op jit(solution)/shard_map/total/pallas_call | solution.py:222
  35.3 13.6 %all-to-all-start.1 = ((f32[128,1,128]{2,1,0:T(1,128)}), f32[128,1,128]{2,1,0:T(1,128)S(1)}, u32[]{:S(2)}, u32[]{:S(2)}) async-start(f32[128,1,128]{2,1,0:T(1,128)} %bitcast.2), calls=%async_computation.1 | async-start | bytes 131072 | tf_op jit(solution)/shard_map/all_to_all | solution.py:228
  48.9 13.0 %all-gather.1 = bf16[4032,128]{1,0:T(8,128)(2,1)S(1)} all-gather(bf16[1008,128]{1,0:T(8,128)(2,1)S(1)} %get-tuple-element.11), channel_id=3, replica_groups=mesh['x'=4,'zh'=2,'c'=2,'y'=8,'zl'=4] {'x'}, dimensions={0}, use_global_device_ids=true | all-gather | bytes 1290240 | tf_op jit(solution)/shard_map/all_gather | solution.py:229
  61.9 0.0 all-to-all-done.1
  61.9 0.0 copy-start
  61.9 0.2 pack.1.refs_2_
  62.1 5.7 %collective-permute-start.2 = (bf16[4144,128]{1,0:T(8,128)(2,1)S(1)}, bf16[4144,128]{1,0:T(8,128)(2,1)S(1)}, u32[]{:S(2)}, u32[]{:S(2)}) collective-permute-start(bf16[4144,128]{1,0:T(8,128)(2,1)S(1)} %pack.1.refs_2_), channel_id=1, source_target_pairs={{0,32},{32,0},{1,33},{33,1},{2,34},{34,2},{3,35},{35,3},{4,36},{36... | collective-permute-start | bytes 3182600 | tf_op jit(solution)/shard_map/ppermute | solution.py:234
  67.8 2.3 %collective-permute-done.2.refs_3_ = bf16[4144,128]{1,0:T(8,128)(2,1)S(1)} collective-permute-done((bf16[4144,128]{1,0:T(8,128)(2,1)S(1)}, bf16[4144,128]{1,0:T(8,128)(2,1)S(1)}, u32[]{:S(2)}, u32[]{:S(2)}) %collective-permute-start.2) | collective-permute-done | bytes 1060896 | tf_op jit(solution)/shard_map/ppermute | solution.py:234
  70.1 0.0 copy-done
  70.1 1.4 %final.1 = (bf16[64,8192]{1,0:T(8,128)(2,1)}, f32[64,512]{1,0:T(8,128)}) custom-call(bf16[64,8192]{1,0:T(8,128)(2,1)S(1)} %copy-done, f32[64,512]{1,0:T(8,128)S(1)} %copy-done.1, bf16[4144,128]{1,0:T(8,128)(2,1)S(1)} %pack.1.refs_2_, bf16[4144,128]{1,0:T(8,128)(2,1)S(1)} %collective-permute-done.2.refs_3_), custom_call_target="tpu_custom_call" | custom-call | tf_op jit(solution)/shard_map/final/pallas_call | solution.py:236
  (1 shorter events, 0.0 us)
Async XLA Ops:
  0.6 11.3 %collective-permute-start = (bf16[1,64,8192]{2,1,0:T(8,128)(2,1)}, bf16[1,64,8192]{2,1,0:T(8,128)(2,1)S(1)}, u32[]{:S(2)}, u32[]{:S(2)}) collective-permute-start(bf16[1,64,8192]{2,1,0:T(8,128)(2,1)} %local_ref.1), channel_id=1, source_target_pairs={{0,32},{32,0},{1,33},{33,1},{2,34},{34,2},{3,35},{35,3},{4,36},{36... | collective-permute-start | bytes 3145736 | tf_op jit(solution)/shard_map/ppermute | solution.py:207
  12.8 3.6 %copy-start.1 = (f32[64,512]{1,0:T(8,128)S(1)}, f32[64,512]{1,0:T(8,128)}, u32[]{:S(2)}) copy-start(f32[64,512]{1,0:T(8,128)} %refs_1_.1) | copy-start | bytes 393220
  12.9 13.0 %all-to-all-start = ((bf16[4,528,128]{2,1,0:T(8,128)(2,1)}), bf16[4,528,128]{2,1,0:T(8,128)(2,1)S(1)}, u32[]{:S(2)}, u32[]{:S(2)}) async-start(bf16[4,528,128]{2,1,0:T(8,128)(2,1)} %pair.1), calls=%async_computation | async-start | bytes 1081344 | tf_op jit(solution)/shard_map/all_to_all | solution.py:215
  16.5 18.0 %collective-permute-start.1 = (bf16[64,512]{1,0:T(8,128)(2,1)S(1)}, bf16[64,512]{1,0:T(8,128)(2,1)S(1)}, u32[]{:S(2)}, u32[]{:S(2)}) collective-permute-start(bf16[64,512]{1,0:T(8,128)(2,1)S(1)} %convert_element_type.3), channel_id=1, source_target_pairs={{0,64},{64,0},{1,65},{65,1},{2,66},{66,2},{3,67},{67,3},{4,68},{68... | collective-permute-start | bytes 196616 | tf_op jit(solution)/shard_map/ppermute | solution.py:206
  35.3 26.6 %all-to-all-start.1 = ((f32[128,1,128]{2,1,0:T(1,128)}), f32[128,1,128]{2,1,0:T(1,128)S(1)}, u32[]{:S(2)}, u32[]{:S(2)}) async-start(f32[128,1,128]{2,1,0:T(1,128)} %bitcast.2), calls=%async_computation.1 | async-start | bytes 131072 | tf_op jit(solution)/shard_map/all_to_all | solution.py:228
  61.9 8.2 %copy-start = (bf16[64,8192]{1,0:T(8,128)(2,1)S(1)}, bf16[64,8192]{1,0:T(8,128)(2,1)}, u32[]{:S(2)}) copy-start(bf16[64,8192]{1,0:T(8,128)(2,1)} %refs_0_.1) | copy-start | bytes 3145732
  62.1 8.0 %collective-permute-start.2 = (bf16[4144,128]{1,0:T(8,128)(2,1)S(1)}, bf16[4144,128]{1,0:T(8,128)(2,1)S(1)}, u32[]{:S(2)}, u32[]{:S(2)}) collective-permute-start(bf16[4144,128]{1,0:T(8,128)(2,1)S(1)} %pack.1.refs_2_), channel_id=1, source_target_pairs={{0,32},{32,0},{1,33},{33,1},{2,34},{34,2},{3,35},{35,3},{4,36},{36... | collective-permute-start | bytes 3182600 | tf_op jit(solution)/shard_map/ppermute | solution.py:234
